TPU v7x, 1024 devices: a whole 4x4x32 slice. The times are simulated.
1024 devices in a mesh: dp: 32 (over z), expert: 32 (over y, x, core).
Axes of the slice: x: 4, y: 4, z: 32, core: 2. Of those that a mesh axis runs over, the one named last changes fastest.
Arguments:
- tokens: bfloat16 [10240, 1664], P('dp', 'expert'), may hold values from -6 to 6
- cotangent: bfloat16 [10240, 1664], P('dp', 'expert'), may hold values from -6 to 6
- gate_values: bfloat16 [10240, 2], P('dp'), may hold values from 0.049804688 to 1
- route_ids: int32 [10240, 2], P('dp'), may hold values from 0 to 31, as said below
- route_slots: int32 [10240, 2], P('dp'), may hold values from 0 to 20, as said below
- kept_mask: int32 [10240, 2], P('dp'), may hold values from 0 to 1, as said below
- weight_in: bfloat16 [32, 1664, 8192], P('expert', None, 'dp'), may hold values from -0.15625 to 0.15625
- weight_out: bfloat16 [32, 8192, 1664], P('expert', 'dp'), may hold values from -0.0625 to 0.0625
Outputs:
- grad_tokens: bfloat16 [10240, 1664], P('dp', 'expert')
- grad_gates: float32 [10240, 2], P('dp')
- grad_in: bfloat16 [32, 1664, 8192], P('expert', None, 'dp')
- grad_out: bfloat16 [32, 8192, 1664], P('expert', 'dp')
Inputs may be any that keep to these rules, and one draw needn't show every extreme that they name: `route_ids`: the two experts of a token differ; which experts are busy differs from group to group of 320 tokens. `route_slots`: within one group of 320 tokens, the kept assignments to one expert hold distinct slots; first choices take slots in priority order, then second choices fill the slots left; a dropped assignment has slot 0. `kept_mask`: an assignment is 0 exactly when its expert's 21 slots of its group were already taken.
All inputs are finite; a program needn't handle non-finite values.
Results may differ from a plain program's by a relative error of at most 0.0057.
Values may be sent and summed in bfloat16 or wider, within the bound.
No kernel may reach another device: no remote copies, remote signals or barrier semaphores. Data moves between devices by JAX's collectives and lax.ppermute only.
A program may use at most 32 MiB of HBM per device.

v0:
```python
import math

import jax
import jax.numpy as jnp
from jax import lax
from jax.sharding import PartitionSpec as P


def gelu_exact(values):
    return 0.5 * values * (1.0 + jax.scipy.special.erf(values / math.sqrt(2.0)))


def gelu_slope(values):
    cumul = 0.5 * (1.0 + jax.scipy.special.erf(values / math.sqrt(2.0)))
    density = jnp.exp(-0.5 * values * values) / math.sqrt(2.0 * math.pi)
    return cumul + values * density


def routing_map(route_ids, route_slots, kept_mask, capacity, slot_total):
    target = route_ids * capacity + route_slots
    columns = jnp.arange(slot_total, dtype=jnp.int32)
    matches = (target[:, :, None] == columns[None, None, :]) & (kept_mask[:, :, None] == 1)
    return matches.astype(jnp.float32)


def body(tokens, cotangent, gate_values, route_ids, route_slots, kept_mask, weight_in, weight_out):
    expert_count = lax.axis_size("expert")
    tok_rows, feature_piece = tokens.shape
    top_count = route_ids.shape[1]
    capacity = (21 * top_count * tok_rows + 20 * expert_count - 1) // (20 * expert_count)
    slot_total = expert_count * capacity
    matches = routing_map(route_ids, route_slots, kept_mask, capacity, slot_total)
    combine_map = jnp.sum(matches, axis=1).astype(jnp.bfloat16)
    row_buffer = jnp.dot(combine_map.T, tokens, preferred_element_type=jnp.float32).astype(
        jnp.bfloat16
    )
    grad_buffer = jnp.dot(combine_map.T, cotangent, preferred_element_type=jnp.float32).astype(
        jnp.bfloat16
    )
    gate_buffer = jnp.einsum("tks,tk->s", matches, gate_values.astype(jnp.float32)).astype(
        jnp.bfloat16
    )
    row_buffer = row_buffer.reshape(expert_count, capacity, feature_piece)
    grad_buffer = grad_buffer.reshape(expert_count, capacity, feature_piece)
    own_gates = lax.dynamic_index_in_dim(
        gate_buffer.reshape(expert_count, capacity), lax.axis_index("expert"), 0, keepdims=False
    )
    arrived_rows, arrived_grads = (
        lax.all_to_all(row_buffer, "expert", split_axis=0, concat_axis=2, tiled=True),
        lax.all_to_all(grad_buffer, "expert", split_axis=0, concat_axis=2, tiled=True),
    )
    arrived_rows = arrived_rows.reshape(capacity, -1)
    arrived_grads = arrived_grads.reshape(capacity, -1)
    expert_rows, expert_grads, expert_gates = (
        lax.all_gather(arrived_rows, "dp", axis=0, tiled=True),
        lax.all_gather(arrived_grads, "dp", axis=0, tiled=True),
        lax.all_gather(own_gates, "dp", axis=0, tiled=True),
    )
    first_weight = weight_in[0]
    second_weight = weight_out[0]
    pre_act = jnp.dot(expert_rows, first_weight, preferred_element_type=jnp.float32)
    hidden = gelu_exact(pre_act)
    grad_raw = jnp.dot(expert_grads, second_weight.T, preferred_element_type=jnp.float32)
    gate_terms = jnp.sum(hidden * grad_raw, axis=1)
    scale = expert_gates.astype(jnp.float32)[:, None]
    grad_pre = (scale * grad_raw * gelu_slope(pre_act)).astype(jnp.bfloat16)
    hidden_low = hidden.astype(jnp.bfloat16)
    scaled_grads = (scale * expert_grads.astype(jnp.float32)).astype(jnp.bfloat16)
    grad_second = jnp.dot(hidden_low.T, scaled_grads, preferred_element_type=jnp.float32).astype(
        jnp.bfloat16
    )
    grad_first = jnp.dot(expert_rows.T, grad_pre, preferred_element_type=jnp.float32).astype(
        jnp.bfloat16
    )
    row_terms = jnp.dot(grad_pre, first_weight.T, preferred_element_type=jnp.float32)
    summed_rows, summed_gates = (
        lax.psum_scatter(row_terms, "dp", scatter_dimension=0, tiled=True),
        lax.psum_scatter(gate_terms, "dp", scatter_dimension=0, tiled=True),
    )
    grad_rows = summed_rows.astype(jnp.bfloat16).reshape(capacity, expert_count, feature_piece)
    gate_copies = jnp.broadcast_to(
        summed_gates.astype(jnp.bfloat16)[:, None], (capacity, expert_count)
    )
    returned_rows, returned_gates = (
        lax.all_to_all(grad_rows, "expert", split_axis=1, concat_axis=0, tiled=True),
        lax.all_to_all(gate_copies, "expert", split_axis=1, concat_axis=0, tiled=True),
    )
    token_grads = jnp.dot(
        combine_map,
        returned_rows.reshape(slot_total, feature_piece),
        preferred_element_type=jnp.float32,
    ).astype(jnp.bfloat16)
    gate_out = jnp.einsum(
        "tks,s->tk", matches, returned_gates.reshape(slot_total).astype(jnp.float32)
    )
    return (token_grads, gate_out, grad_first[None], grad_second[None])


def solution(mesh):
    return jax.shard_map(
        body,
        mesh=mesh,
        in_specs=(
            P("dp", "expert"),
            P("dp", "expert"),
            P("dp", None),
            P("dp", None),
            P("dp", None),
            P("dp", None),
            P("expert", None, "dp"),
            P("expert", "dp", None),
        ),
        out_specs=(
            P("dp", "expert"),
            P("dp", None),
            P("expert", None, "dp"),
            P("expert", "dp", None),
        ),
        check_vma=False,
    )
```

profile of v0, /device:TPU:1, one launch (start us, length us, event | category | flops | bytes accessed | tf_op | source)
XLA Modules:
  0.0 492.7 jit_solution(6694931320374983568)
XLA Ops:
  7.2 0.0 copy-start
  7.2 0.0 copy-start.6
  7.2 0.0 all-gather.8.cloned.1.call-start
  7.2 0.8 broadcast_compare_fusion
  8.0 0.7 multiply_add_fusion
  8.7 0.4 convert_reduce_fusion
  9.1 0.0 copy-start.1
  9.1 1.0 convolution_convert_fusion.2
  10.2 0.2 copy.30
  10.4 0.1 reshape.51
  10.4 0.2 reshape.80
  10.6 24.2 %all_to_all.58 = bf16[32,2,546]{2,1,0:T(2,128)(2,1)S(1)} all-to-all(bf16[32,2,546]{2,1,0:T(2,128)(2,1)S(1)} %reshape.80), channel_id=1, replica_groups=mesh['dp'=32,'expert'=32] {'expert'}, dimensions={0} | all-to-all | bytes 139776 | tf_op jit(solution)/shard_map/all_to_all | solution.py:49
  34.9 0.3 reshape.81
  35.2 0.9 reshape.63
  36.1 0.0 all-gather.8.cloned.1.call-update
  36.1 0.0 all-gather.6.cloned.1.call-start
  36.1 0.0 copy-done.6
  36.2 0.2 convolution_convert_fusion.3
  36.4 0.2 copy.28
  36.5 0.1 reshape.49
  36.6 0.2 reshape.82
  36.8 10.9 %all_to_all.59 = bf16[32,2,546]{2,1,0:T(2,128)(2,1)S(1)} all-to-all(bf16[32,2,546]{2,1,0:T(2,128)(2,1)S(1)} %reshape.82), channel_id=1, replica_groups=mesh['dp'=32,'expert'=32] {'expert'}, dimensions={0} | all-to-all | bytes 139776 | tf_op jit(solution)/shard_map/all_to_all | solution.py:50
  47.7 0.3 reshape.83
  48.0 0.0 copy-done.1
  48.1 0.9 reshape.61
  49.0 0.0 all-gather.6.cloned.1.call-update
  49.0 0.0 copy-done.7
  49.0 0.8 fusion.8
  49.8 0.1 reshape.48
  49.9 1.4 fusion.35
  52.0 0.2 dynamic-update-slice
  52.2 48.7 %all-reduce = bf16[672]{0:T(1024)(128)(2,1)S(1)} all-reduce(bf16[672]{0:T(1024)(128)(2,1)S(1)} %dynamic-update-slice), channel_id=2, replica_groups=mesh['dp'=32,'expert'=32] {'dp'}, use_global_device_ids=true, to_apply=%add | all-reduce | flops 672 | bytes 2688
  101.6 49.8 %all-gather.8.cloned.1.call-done = bf16[32,21,1664]{2,1,0:T(8,128)(2,1)} async-done(((bf16[1,21,1664]{2,1,0:T(8,128)(2,1)}), bf16[32,21,1664]{2,1,0:T(8,128)(2,1)}) %all-gather.8.cloned.1.call-update) | async-done | bytes 2236432 | tf_op jit(solution)/shard_map/all_gather | solution.py:55
  151.4 2.8 reshape.64
  154.2 0.0 copy-done
  154.2 0.0 copy-start.4
  154.2 1.6 fusion.17
  155.8 130.4 %all-gather.6.cloned.1.call-done = bf16[32,21,1664]{2,1,0:T(8,128)(2,1)} async-done(((bf16[1,21,1664]{2,1,0:T(8,128)(2,1)}), bf16[32,21,1664]{2,1,0:T(8,128)(2,1)}) %all-gather.6.cloned.1.call-update) | async-done | bytes 2236432 | tf_op jit(solution)/shard_map/all_gather | solution.py:56
  286.2 2.8 reshape.62
  289.0 0.0 copy-start.3
  289.0 2.4 multiply_reduce_fusion
  291.4 0.0 copy-done.3
  291.4 1.9 fusion.1
  293.3 2.0 fusion
  295.3 3.1 fusion.15
  298.4 115.3 %all-reduce.5 = (bf16[672,1664]{1,0:T(8,128)(2,1)}, bf16[672]{0:T(1024)(128)(2,1)S(1)}) all-reduce(f32[672,1664]{1,0:T(8,128)} %fusion.15, f32[672]{0:T(1024)S(1)} %get-tuple-element.8), channel_id=3, replica_groups=mesh['dp'=32,'expert'=32] {'dp'}, use_global_device_ids=true, to_apply=%region_1.2.clone | all-reduce | flops 1118880 | bytes 6713280
  413.7 0.1 dynamic-slice.7
  413.8 0.6 broadcast_in_dim.6
  414.4 51.7 %all-to-all-start.3 = ((bf16[21,32,1]{0,2,1:T(2,128)(2,1)}), bf16[21,32,1]{0,2,1:T(2,128)(2,1)S(1)}, u32[]{:S(2)}, u32[]{:S(2)}) async-start(bf16[21,32,1]{0,2,1:T(2,128)(2,1)} %broadcast_in_dim.6), calls=%async_computation.3 | async-start | bytes 32768 | tf_op jit(solution)/shard_map/all_to_all | solution.py:86
  466.1 0.9 dynamic-slice_convert_fusion
  467.0 0.5 reshape.53
  467.5 0.1 copy.38
  467.6 0.8 reshape.84
  468.4 4.5 all-to-all-done.3
  472.9 4.2 all-to-all-start.2
  477.1 0.1 bitcast_reduce_fusion
  477.2 0.1 reshape.73
  477.3 0.8 fusion.4
  478.1 0.7 copy.34
  478.8 5.7 %all-to-all-done.2 = bf16[32,2,546]{2,1,0:T(2,128)(2,1)S(1)} async-done(((bf16[32,2,546]{2,1,0:T(2,128)(2,1)}), bf16[32,2,546]{2,1,0:T(2,128)(2,1)S(1)}, u32[]{:S(2)}, u32[]{:S(2)}) %all-to-all-start.2) | async-done | bytes 69920 | tf_op jit(solution)/shard_map/all_to_all | solution.py:85
  484.6 0.3 reshape.85
  484.9 0.1 reshape.54
  484.9 0.0 copy-done.2
  485.0 0.9 convolution_convert_fusion.4
  (11 shorter events, 0.1 us)
Async XLA Ops:
  7.2 147.0 %copy-start = (bf16[1,1664,256]{2,1,0:T(8,128)(2,1)S(1)}, bf16[1,1664,256]{2,1,0:T(8,128)(2,1)}, u32[]{:S(2)}) copy-start(bf16[1,1664,256]{2,1,0:T(8,128)(2,1)} %param.14) | copy-start | bytes 2555908
  7.2 29.0 %copy-start.6 = (bf16[320,52]{0,1:T(8,128)(2,1)S(1)}, bf16[320,52]{0,1:T(8,128)(2,1)}, u32[]{:S(2)}) copy-start(bf16[320,52]{0,1:T(8,128)(2,1)} %param.9) | copy-start | bytes 99844
  7.2 144.2 %all-gather.8.cloned.1.call-start = ((), (), s32[]{:S(2)}) async-start(), calls=%async_computation.5 | async-start | bytes 2635776 | tf_op jit(solution)/shard_map/all_gather | solution.py:55
  9.1 38.9 %copy-start.1 = (bf16[320,672]{1,0:T(8,128)(2,1)}, bf16[320,672]{1,0:T(8,128)(2,1)S(1)}, u32[]{:S(2)}) copy-start(bf16[320,672]{1,0:T(8,128)(2,1)S(1)} %convert_reduce_fusion) | copy-start | bytes 1290244
  10.3 38.7 %copy-start.7 = (bf16[320,2]{0,1:T(2,128)(2,1)S(1)}, bf16[320,2]{0,1:T(2,128)(2,1)}, u32[]{:S(2)}) copy-start(bf16[320,2]{0,1:T(2,128)(2,1)} %param.10) | copy-start | bytes 3844
  36.1 250.1 %all-gather.6.cloned.1.call-start = ((), (), s32[]{:S(2)}) async-start(), calls=%async_computation.4 | async-start | bytes 2635776 | tf_op jit(solution)/shard_map/all_gather | solution.py:56
  154.2 1.7 copy-start.4
  289.0 2.4 copy-start.3
  291.4 1.9 copy-start.5
  413.7 71.2 %copy-start.2 = (bf16[320,672]{1,0:T(8,128)(2,1)S(1)}, bf16[320,672]{1,0:T(8,128)(2,1)}, u32[]{:S(2)}) copy-start(bf16[320,672]{1,0:T(8,128)(2,1)} %copy-done.1) | copy-start | bytes 1290244
  414.4 58.5 %all-to-all-start.3 = ((bf16[21,32,1]{0,2,1:T(2,128)(2,1)}), bf16[21,32,1]{0,2,1:T(2,128)(2,1)S(1)}, u32[]{:S(2)}, u32[]{:S(2)}) async-start(bf16[21,32,1]{0,2,1:T(2,128)(2,1)} %broadcast_in_dim.6), calls=%async_computation.3 | async-start | bytes 32768 | tf_op jit(solution)/shard_map/all_to_all | solution.py:86
  472.9 11.6 %all-to-all-start.2 = ((bf16[32,2,546]{2,1,0:T(2,128)(2,1)}), bf16[32,2,546]{2,1,0:T(2,128)(2,1)S(1)}, u32[]{:S(2)}, u32[]{:S(2)}) async-start(bf16[32,2,546]{2,1,0:T(2,128)(2,1)} %reshape.84), calls=%async_computation.2 | async-start | bytes 163840 | tf_op jit(solution)/shard_map/all_to_all | solution.py:85
Sparse Core Ops, SparseCore 0:
  36.2 115.0 all-gather.7
  154.6 131.5 all-gather.5
where the time goes:
time: 493 us
  blocking collectives  199 us (40%)
  waiting for transfers between devices  190 us (39%)
  starting transfers between devices  55.9 us (11%)
  between operations  15.6 us (3%)
  local copies, waits for them, and re-layouts  14.9 us (3%)
  matrix products  14.7 us (3%)
    unnamed x2, blocking collectives  164 us
    all_gather x1, waiting for transfers between devices, body(): lax.all_gather(arrived_grads, 'dp', axis=0, tiled=True)  130 us
    all_to_all x1, starting transfers between devices, body(): lax.all_to_all(gate_copies, 'expert', split_axis=1, concat_axis=0, tiled=...  51.7 us
    all_gather x1, waiting for transfers between devices, body(): lax.all_gather(arrived_rows, 'dp', axis=0, tiled=True)  49.8 us
    all_to_all x1, blocking collectives, body(): lax.all_to_all(row_buffer, 'expert', split_axis=0, concat_axis=2, tiled=T...  24.2 us
    unnamed x31, local copies, waits for them, and re-layouts  11.2 us
    all_to_all x1, blocking collectives, body(): lax.all_to_all(grad_buffer, 'expert', split_axis=0, concat_axis=2, tiled=...  10.9 us
  transfers between devices with their start and end apart: 4, of which 4 were waited for; matrix products, arithmetic and copies ran while one was open for 3% of the time, Pallas kernels for 0%

commit v1 on v0

v1 whole, which is shorter than its diff:
```python
import math

import jax
import jax.numpy as jnp
from jax import lax
from jax.sharding import PartitionSpec as P

BF16 = jnp.bfloat16
F32 = jnp.float32


def gelu_pair(values):
    cumul = 0.5 * (1.0 + lax.erf(values * (1.0 / math.sqrt(2.0))))
    density = jnp.exp(-0.5 * values * values) * (1.0 / math.sqrt(2.0 * math.pi))
    return values * cumul, cumul + values * density


def dot(left, right, dims):
    return lax.dot_general(left, right, ((dims[0], dims[1]), ((), ())), preferred_element_type=F32)


def body(tokens, cotangent, gate_values, route_ids, route_slots, kept_mask, weight_in, weight_out):
    experts = lax.axis_size("expert")
    dp = lax.axis_size("dp")
    half = dp // 2
    tok_rows, piece = tokens.shape
    width = piece * experts
    top = route_ids.shape[1]
    cap = (21 * top * tok_rows + 20 * experts - 1) // (20 * experts)
    pad = (cap + 1 + 7) // 8 * 8
    ring_cut = max(128, width * 5 // 8 // 128 * 128)
    me = lax.axis_index("expert")
    spot = lax.axis_index("dp") // 2
    mates = [(i, i ^ 1) for i in range(dp)]
    back = [(i, (i - 2) % dp) for i in range(dp)]
    groups = [list(range(0, dp, 2)), list(range(1, dp, 2))]

    own_in, own_out = weight_in[0], weight_out[0]
    mate_in = lax.ppermute(own_in, "dp", mates)
    mate_out = lax.ppermute(own_out, "dp", mates)

    kept = kept_mask == 1
    target = jnp.where(kept, route_ids * pad + route_slots, -1)
    slots = jnp.arange(experts * pad, dtype=jnp.int32)
    both = jnp.concatenate([tokens, cotangent], axis=1)
    spread = jnp.zeros((experts * pad, tok_rows), jnp.bool_)
    for k in range(top):
        spread = spread | (slots[:, None] == target[None, :, k])
    placed = dot(spread.astype(BF16), both, ((1,), (0,))).astype(BF16)
    placed = placed.reshape(experts, pad, 2 * piece)
    arrived = lax.all_to_all(placed, "expert", split_axis=0, concat_axis=0, tiled=True)
    arrived = arrived.reshape(experts, pad, 2, piece).transpose(2, 1, 0, 3).reshape(2, pad, width)

    own_slots = jnp.arange(width, dtype=jnp.int32)
    hit = (target[:, :, None] == me * pad + own_slots[None, None, :]) & (own_slots < cap)[None, None, :]
    own_gates = jnp.sum(jnp.where(hit, gate_values.astype(F32)[:, :, None], 0.0), axis=(0, 1))
    spare = lax.broadcasted_iota(jnp.int32, (pad, width), 0) == cap
    row_block = jnp.where(spare, own_gates.astype(BF16)[None, :], arrived[0])
    grad_block = arrived[1]

    row_all = lax.all_gather(row_block, "dp", axis=0, axis_index_groups=groups)
    grad_all = jnp.zeros((half, pad, width), BF16)
    moving = grad_block
    for step in range(half):
        grad_all = lax.dynamic_update_slice(grad_all, moving[None], ((spot + step) % half, 0, 0))
        if step < half - 1:
            moving = lax.ppermute(moving, "dp", back)
    gates = jnp.pad(row_all[:, cap, :cap].astype(F32), ((0, 0), (0, pad - cap))).reshape(half * pad, 1)
    rows = row_all.reshape(half * pad, width)
    grads = grad_all.reshape(half * pad, width)

    scaled = (gates * grads.astype(F32)).astype(BF16)
    gate_terms = jnp.zeros((half * pad,), F32)
    slopes, lows = [], []
    for first, second in ((own_in, own_out), (mate_in, mate_out)):
        pre = dot(rows, first, ((1,), (0,)))
        raw = dot(grads, second, ((1,), (1,)))
        hidden, slope = gelu_pair(pre)
        gate_terms = gate_terms + jnp.sum(hidden * raw, axis=1)
        slopes.append((gates * raw * slope).astype(BF16))
        lows.append(hidden.astype(BF16))
    row_terms = dot(slopes[0], own_in, ((1,), (1,))) + dot(slopes[1], mate_in, ((1,), (1,)))
    row_terms = row_terms.reshape(half, pad, width)
    gate_terms = jnp.pad(gate_terms.reshape(half, pad)[:, :cap], ((0, 0), (0, ring_cut - cap)))
    spare_row = lax.broadcasted_iota(jnp.int32, (1, pad, 1), 1) == cap
    near = jnp.where(spare_row, gate_terms[:, None, :], row_terms[:, :, :ring_cut])
    far = row_terms[:, :, ring_cut:]

    summed = lax.psum_scatter(near, "dp", scatter_dimension=0, axis_index_groups=groups)
    moving = lax.dynamic_index_in_dim(far, (spot + 1) % half, 0, keepdims=False)
    for step in range(half - 1):
        moving = lax.ppermute(moving, "dp", back)
        moving = moving + lax.dynamic_index_in_dim(far, (spot + 2 + step) % half, 0, keepdims=False)

    mate_first = lax.ppermute(dot(rows, slopes[1], ((0,), (0,))).astype(BF16), "dp", mates)
    mate_second = lax.ppermute(dot(lows[1], scaled, ((0,), (0,))).astype(BF16), "dp", mates)
    grad_first = (dot(rows, slopes[0], ((0,), (0,))) + mate_first.astype(F32)).astype(BF16)
    grad_second = (dot(lows[0], scaled, ((0,), (0,))) + mate_second.astype(F32)).astype(BF16)

    slot_gates = jnp.pad(summed[cap, :cap].astype(BF16), (0, piece - cap))
    grad_rows = jnp.concatenate([summed, moving], axis=1).astype(BF16).reshape(pad, experts, piece)
    grad_rows = grad_rows.transpose(1, 0, 2)
    spare_slot = lax.broadcasted_iota(jnp.int32, (1, pad, 1), 1) == cap
    grad_rows = jnp.where(spare_slot, slot_gates[None, None, :], grad_rows)
    returned = lax.all_to_all(grad_rows, "expert", split_axis=0, concat_axis=0, tiled=True)
    gates_back = jnp.pad(returned[:, cap, :cap], ((0, 0), (0, pad - cap))).reshape(experts * pad)
    returned = returned.reshape(experts * pad, piece)
    gather = jnp.zeros((tok_rows, experts * pad), jnp.bool_)
    gate_out = []
    for k in range(top):
        match = target[:, k, None] == slots[None, :]
        gather = gather | match
        gate_out.append(jnp.sum(jnp.where(match, gates_back.astype(F32)[None, :], 0.0), axis=1))
    token_grads = dot(gather.astype(BF16), returned, ((1,), (0,))).astype(BF16)
    return token_grads, jnp.stack(gate_out, axis=1), grad_first[None], grad_second[None]


def solution(mesh):
    return jax.shard_map(
        body,
        mesh=mesh,
        in_specs=(
            P("dp", "expert"),
            P("dp", "expert"),
            P("dp", None),
            P("dp", None),
            P("dp", None),
            P("dp", None),
            P("expert", None, "dp"),
            P("expert", "dp", None),
        ),
        out_specs=(
            P("dp", "expert"),
            P("dp", None),
            P("expert", None, "dp"),
            P("expert", "dp", None),
        ),
        check_vma=False,
    )
```

time: 493 us -> 444 us (0.901)
  starting transfers between devices: 55.9 us -> 293 us
  blocking collectives: 199 us -> 0 us
  waiting for transfers between devices: 190 us -> 86.4 us
  other arithmetic: 1.88 us -> 15.7 us
  local copies, waits for them, and re-layouts: 14.9 us -> 5.58 us
  matrix products: 14.7 us -> 23.9 us
    ppermute x0 -> x34, starting transfers between devices: none -> 243 us  [the longest x30 176 us: body(): moving = lax.ppermute(moving, 'dp', back)]
    all_gather x2 -> x1, waiting for transfers between devices: 180 us -> 0.02 us  [body(): row_all = lax.all_gather(row_block, 'dp', axis=0, axis_index_groups=groups)]
    unnamed x2 -> x0, blocking collectives: 164 us -> none
    ppermute x0 -> x34, waiting for transfers between devices: none -> 57.7 us  [the longest x30 57.7 us: body(): moving = lax.ppermute(moving, 'dp', back)]
    all_to_all x2 -> x0, blocking collectives: 35.2 us -> none  [the longest x1 24.2 us: body(): lax.all_to_all(row_buffer, 'expert', split_axis=0, concat_axis=2, tiled=T...]
    reduce_scatter x0 -> x1, waiting for transfers between devices: none -> 22.3 us  [body(): lax.psum_scatter(near, 'dp', scatter_dimension=0, axis_index_groups=groups)]
    unnamed x31 -> x18, local copies, waits for them, and re-layouts: 11.2 us -> 1.33 us
    dot_general x10 -> x12, matrix products: 14.7 us -> 23.9 us  [dot(): lax.dot_general(left, right, ((dims[0], dims[1]), ((), ())), preferred_el...]
  transfers between devices with their start and end apart: 4 -> 38, of which waited for: 4 -> 30; matrix products, arithmetic and copies ran while one was open for 3% -> 8% of each run, Pallas kernels for 0% -> 0%
where the time goes in v1:
time: 444 us; the launch traced here: 440 us
  starting transfers between devices  293 us (66%)
  waiting for transfers between devices  86.4 us (19%)
  matrix products  23.9 us (5%)
  other arithmetic  15.7 us (4%)
  between operations  15.2 us (3%)
  local copies, waits for them, and re-layouts  5.58 us (1%)
    ppermute x30, starting transfers between devices, body(): moving = lax.ppermute(moving, 'dp', back)  176 us
    ppermute x30, waiting for transfers between devices, body(): moving = lax.ppermute(moving, 'dp', back)  57.7 us
    ppermute x1, starting transfers between devices, body(): lax.ppermute(dot(rows, slopes[1], ((0,), (0,))).astype(BF16), 'dp', mates)  44.3 us
    all_to_all x1, starting transfers between devices, body(): lax.all_to_all(grad_rows, 'expert', split_axis=0, concat_axis=0, tiled=True)  32 us
    dot_general x12, matrix products, dot(): lax.dot_general(left, right, ((dims[0], dims[1]), ((), ())), preferred_el...  23.9 us
    reduce_scatter x1, waiting for transfers between devices, body(): lax.psum_scatter(near, 'dp', scatter_dimension=0, axis_index_groups=groups)  22.3 us
    ppermute x1, starting transfers between devices, body(): lax.ppermute(dot(lows[1], scaled, ((0,), (0,))).astype(BF16), 'dp', mates)  17.7 us
    all_to_all x1, starting transfers between devices, body(): lax.all_to_all(placed, 'expert', split_axis=0, concat_axis=0, tiled=True)  17.7 us
  transfers between devices with their start and end apart: 38, of which 30 were waited for; matrix products, arithmetic and copies ran while one was open for 8% of the time, Pallas kernels for 0%

profile of v1, /device:TPU:1, one launch (start us, length us, event | category | flops | bytes accessed | tf_op | source)
XLA Modules:
  0.0 439.8 jit_solution(6812489319702846587)
XLA Ops:
  10.0 17.7 %all-to-all-start = ((bf16[32,24,104]{2,1,0:T(8,128)(2,1)}), bf16[32,24,104]{2,1,0:T(8,128)(2,1)S(1)}, u32[]{:S(2)}, u32[]{:S(2)}) async-start(bf16[32,24,104]{2,1,0:T(8,128)(2,1)} %bitcast), calls=%async_computation | async-start | bytes 393216 | tf_op jit(solution)/shard_map/all_to_all | solution.py:51
  27.7 1.9 collective-permute-start.15
  29.7 3.4 collective-permute-start.16
  36.9 9.6 %collective-permute-start = (bf16[24,1664]{1,0:T(8,128)(2,1)S(1)}, bf16[24,1664]{1,0:T(8,128)(2,1)S(1)}, u32[]{:S(2)}, u32[]{:S(2)}) collective-permute-start(bf16[24,1664]{1,0:T(8,128)(2,1)S(1)} %squeeze.68), channel_id=1, source_target_pairs={{0,960},{32,992},{64,0},{96,32},{128,64},{160,96},{192,128},{224,1... | collective-permute-start | bytes 239624 | tf_op jit(solution)/shard_map/ppermute | solution.py:67
  48.2 6.2 %collective-permute-start.1 = (bf16[24,1664]{1,0:T(8,128)(2,1)S(1)}, bf16[24,1664]{1,0:T(8,128)(2,1)S(1)}, u32[]{:S(2)}, u32[]{:S(2)}) collective-permute-start(bf16[24,1664]{1,0:T(8,128)(2,1)S(1)} %collective-permute-done), channel_id=1, source_target_pairs={{0,960},{32,992},{64,0},{96,32},{128,64},{160,96},{192,128},{224,1... | collective-permute-start | bytes 239624 | tf_op jit(solution)/shard_map/ppermute | solution.py:67
  55.9 5.9 %collective-permute-start.2 = (bf16[24,1664]{1,0:T(8,128)(2,1)S(1)}, bf16[24,1664]{1,0:T(8,128)(2,1)S(1)}, u32[]{:S(2)}, u32[]{:S(2)}) collective-permute-start(bf16[24,1664]{1,0:T(8,128)(2,1)S(1)} %collective-permute-done.1), channel_id=1, source_target_pairs={{0,960},{32,992},{64,0},{96,32},{128,64},{160,96},{192,128},{224,1... | collective-permute-start | bytes 239624 | tf_op jit(solution)/shard_map/ppermute | solution.py:67
  63.3 5.9 %collective-permute-start.3 = (bf16[24,1664]{1,0:T(8,128)(2,1)S(1)}, bf16[24,1664]{1,0:T(8,128)(2,1)S(1)}, u32[]{:S(2)}, u32[]{:S(2)}) collective-permute-start(bf16[24,1664]{1,0:T(8,128)(2,1)S(1)} %collective-permute-done.2), channel_id=1, source_target_pairs={{0,960},{32,992},{64,0},{96,32},{128,64},{160,96},{192,128},{224,1... | collective-permute-start | bytes 239624 | tf_op jit(solution)/shard_map/ppermute | solution.py:67
  69.2 1.9 collective-permute-done.3
  71.1 5.4 %collective-permute-start.4 = (bf16[24,1664]{1,0:T(8,128)(2,1)S(1)}, bf16[24,1664]{1,0:T(8,128)(2,1)S(1)}, u32[]{:S(2)}, u32[]{:S(2)}) collective-permute-start(bf16[24,1664]{1,0:T(8,128)(2,1)S(1)} %collective-permute-done.3), channel_id=1, source_target_pairs={{0,960},{32,992},{64,0},{96,32},{128,64},{160,96},{192,128},{224,1... | collective-permute-start | bytes 239624 | tf_op jit(solution)/shard_map/ppermute | solution.py:67
  76.6 2.4 collective-permute-done.4
  79.0 6.3 %collective-permute-start.5 = (bf16[24,1664]{1,0:T(8,128)(2,1)S(1)}, bf16[24,1664]{1,0:T(8,128)(2,1)S(1)}, u32[]{:S(2)}, u32[]{:S(2)}) collective-permute-start(bf16[24,1664]{1,0:T(8,128)(2,1)S(1)} %collective-permute-done.4), channel_id=1, source_target_pairs={{0,960},{32,992},{64,0},{96,32},{128,64},{160,96},{192,128},{224,1... | collective-permute-start | bytes 239624 | tf_op jit(solution)/shard_map/ppermute | solution.py:67
  85.3 2.6 collective-permute-done.5
  87.9 6.5 %collective-permute-start.6 = (bf16[24,1664]{1,0:T(8,128)(2,1)S(1)}, bf16[24,1664]{1,0:T(8,128)(2,1)S(1)}, u32[]{:S(2)}, u32[]{:S(2)}) collective-permute-start(bf16[24,1664]{1,0:T(8,128)(2,1)S(1)} %collective-permute-done.5), channel_id=1, source_target_pairs={{0,960},{32,992},{64,0},{96,32},{128,64},{160,96},{192,128},{224,1... | collective-permute-start | bytes 239624 | tf_op jit(solution)/shard_map/ppermute | solution.py:67
  94.4 2.1 collective-permute-done.6
  96.5 6.5 %collective-permute-start.7 = (bf16[24,1664]{1,0:T(8,128)(2,1)S(1)}, bf16[24,1664]{1,0:T(8,128)(2,1)S(1)}, u32[]{:S(2)}, u32[]{:S(2)}) collective-permute-start(bf16[24,1664]{1,0:T(8,128)(2,1)S(1)} %collective-permute-done.6), channel_id=1, source_target_pairs={{0,960},{32,992},{64,0},{96,32},{128,64},{160,96},{192,128},{224,1... | collective-permute-start | bytes 239624 | tf_op jit(solution)/shard_map/ppermute | solution.py:67
  103.1 2.8 collective-permute-done.7
  105.9 6.6 %collective-permute-start.8 = (bf16[24,1664]{1,0:T(8,128)(2,1)S(1)}, bf16[24,1664]{1,0:T(8,128)(2,1)S(1)}, u32[]{:S(2)}, u32[]{:S(2)}) collective-permute-start(bf16[24,1664]{1,0:T(8,128)(2,1)S(1)} %collective-permute-done.7), channel_id=1, source_target_pairs={{0,960},{32,992},{64,0},{96,32},{128,64},{160,96},{192,128},{224,1... | collective-permute-start | bytes 239624 | tf_op jit(solution)/shard_map/ppermute | solution.py:67
  112.5 4.2 collective-permute-done.8
  116.7 6.6 %collective-permute-start.9 = (bf16[24,1664]{1,0:T(8,128)(2,1)S(1)}, bf16[24,1664]{1,0:T(8,128)(2,1)S(1)}, u32[]{:S(2)}, u32[]{:S(2)}) collective-permute-start(bf16[24,1664]{1,0:T(8,128)(2,1)S(1)} %collective-permute-done.8), channel_id=1, source_target_pairs={{0,960},{32,992},{64,0},{96,32},{128,64},{160,96},{192,128},{224,1... | collective-permute-start | bytes 239624 | tf_op jit(solution)/shard_map/ppermute | solution.py:67
  123.4 3.7 collective-permute-done.9
  127.1 6.4 %collective-permute-start.10 = (bf16[24,1664]{1,0:T(8,128)(2,1)S(1)}, bf16[24,1664]{1,0:T(8,128)(2,1)S(1)}, u32[]{:S(2)}, u32[]{:S(2)}) collective-permute-start(bf16[24,1664]{1,0:T(8,128)(2,1)S(1)} %collective-permute-done.9), channel_id=1, source_target_pairs={{0,960},{32,992},{64,0},{96,32},{128,64},{160,96},{192,128},{224,1... | collective-permute-start | bytes 239624 | tf_op jit(solution)/shard_map/ppermute | solution.py:67
  133.6 3.1 collective-permute-done.10
  136.7 6.3 %collective-permute-start.11 = (bf16[24,1664]{1,0:T(8,128)(2,1)S(1)}, bf16[24,1664]{1,0:T(8,128)(2,1)S(1)}, u32[]{:S(2)}, u32[]{:S(2)}) collective-permute-start(bf16[24,1664]{1,0:T(8,128)(2,1)S(1)} %collective-permute-done.10), channel_id=1, source_target_pairs={{0,960},{32,992},{64,0},{96,32},{128,64},{160,96},{192,128},{224,1... | collective-permute-start | bytes 239624 | tf_op jit(solution)/shard_map/ppermute | solution.py:67
  143.1 2.9 collective-permute-done.11
  145.9 6.3 %collective-permute-start.12 = (bf16[24,1664]{1,0:T(8,128)(2,1)S(1)}, bf16[24,1664]{1,0:T(8,128)(2,1)S(1)}, u32[]{:S(2)}, u32[]{:S(2)}) collective-permute-start(bf16[24,1664]{1,0:T(8,128)(2,1)S(1)} %collective-permute-done.11), channel_id=1, source_target_pairs={{0,960},{32,992},{64,0},{96,32},{128,64},{160,96},{192,128},{224,1... | collective-permute-start | bytes 239624 | tf_op jit(solution)/shard_map/ppermute | solution.py:67
  152.3 2.3 collective-permute-done.12
  154.6 6.3 %collective-permute-start.13 = (bf16[24,1664]{1,0:T(8,128)(2,1)S(1)}, bf16[24,1664]{1,0:T(8,128)(2,1)S(1)}, u32[]{:S(2)}, u32[]{:S(2)}) collective-permute-start(bf16[24,1664]{1,0:T(8,128)(2,1)S(1)} %collective-permute-done.12), channel_id=1, source_target_pairs={{0,960},{32,992},{64,0},{96,32},{128,64},{160,96},{192,128},{224,1... | collective-permute-start | bytes 239624 | tf_op jit(solution)/shard_map/ppermute | solution.py:67
  161.0 2.4 collective-permute-done.13
  163.3 6.3 %collective-permute-start.14 = (bf16[24,1664]{1,0:T(8,128)(2,1)S(1)}, bf16[24,1664]{1,0:T(8,128)(2,1)S(1)}, u32[]{:S(2)}, u32[]{:S(2)}) collective-permute-start(bf16[24,1664]{1,0:T(8,128)(2,1)S(1)} %collective-permute-done.13), channel_id=1, source_target_pairs={{0,960},{32,992},{64,0},{96,32},{128,64},{160,96},{192,128},{224,1... | collective-permute-start | bytes 239624 | tf_op jit(solution)/shard_map/ppermute | solution.py:67
  169.7 2.3 collective-permute-done.14
  173.0 2.3 fusion.40
  175.3 1.8 fusion.50
  177.2 1.8 multiply_reduce_fusion.1
  179.0 2.0 fusion.38
  181.0 1.8 multiply_reduce_fusion
  182.8 2.0 convolution_add_fusion
  185.0 6.4 %collective-permute-start.17 = (f32[24,640]{1,0:T(8,128)S(1)}, f32[24,640]{1,0:T(8,128)S(1)}, u32[]{:S(2)}, u32[]{:S(2)}) collective-permute-start(f32[24,640]{1,0:T(8,128)S(1)} %dynamic-slice_bitcast_fusion), channel_id=1, source_target_pairs={{0,960},{32,992},{64,0},{96,32},{128,64},{160,96},{192,128},{224,1... | collective-permute-start | bytes 184328 | tf_op jit(solution)/shard_map/ppermute | solution.py:92
  193.0 5.9 %collective-permute-start.18 = (f32[24,640]{1,0:T(8,128)S(1)}, f32[24,640]{1,0:T(8,128)S(1)}, u32[]{:S(2)}, u32[]{:S(2)}) collective-permute-start(f32[24,640]{1,0:T(8,128)S(1)} %bitcast_add_fusion.14), channel_id=1, source_target_pairs={{0,960},{32,992},{64,0},{96,32},{128,64},{160,96},{192,128},{224,1... | collective-permute-start | bytes 184328 | tf_op jit(solution)/shard_map/ppermute | solution.py:92
  200.3 5.9 %collective-permute-start.19 = (f32[24,640]{1,0:T(8,128)S(1)}, f32[24,640]{1,0:T(8,128)S(1)}, u32[]{:S(2)}, u32[]{:S(2)}) collective-permute-start(f32[24,640]{1,0:T(8,128)S(1)} %bitcast_add_fusion.13), channel_id=1, source_target_pairs={{0,960},{32,992},{64,0},{96,32},{128,64},{160,96},{192,128},{224,1... | collective-permute-start | bytes 184328 | tf_op jit(solution)/shard_map/ppermute | solution.py:92
  206.2 2.0 collective-permute-done.19
  208.3 5.9 %collective-permute-start.20 = (f32[24,640]{1,0:T(8,128)S(1)}, f32[24,640]{1,0:T(8,128)S(1)}, u32[]{:S(2)}, u32[]{:S(2)}) collective-permute-start(f32[24,640]{1,0:T(8,128)S(1)} %bitcast_add_fusion.12), channel_id=1, source_target_pairs={{0,960},{32,992},{64,0},{96,32},{128,64},{160,96},{192,128},{224,1... | collective-permute-start | bytes 184328 | tf_op jit(solution)/shard_map/ppermute | solution.py:92
  214.2 2.2 collective-permute-done.20
  216.4 5.9 %collective-permute-start.21 = (f32[24,640]{1,0:T(8,128)S(1)}, f32[24,640]{1,0:T(8,128)S(1)}, u32[]{:S(2)}, u32[]{:S(2)}) collective-permute-start(f32[24,640]{1,0:T(8,128)S(1)} %bitcast_add_fusion.11), channel_id=1, source_target_pairs={{0,960},{32,992},{64,0},{96,32},{128,64},{160,96},{192,128},{224,1... | collective-permute-start | bytes 184328 | tf_op jit(solution)/shard_map/ppermute | solution.py:92
  223.6 6.7 %collective-permute-start.22 = (f32[24,640]{1,0:T(8,128)S(1)}, f32[24,640]{1,0:T(8,128)S(1)}, u32[]{:S(2)}, u32[]{:S(2)}) collective-permute-start(f32[24,640]{1,0:T(8,128)S(1)} %bitcast_add_fusion.10), channel_id=1, source_target_pairs={{0,960},{32,992},{64,0},{96,32},{128,64},{160,96},{192,128},{224,1... | collective-permute-start | bytes 184328 | tf_op jit(solution)/shard_map/ppermute | solution.py:92
  232.4 5.8 %collective-permute-start.23 = (f32[24,640]{1,0:T(8,128)S(1)}, f32[24,640]{1,0:T(8,128)S(1)}, u32[]{:S(2)}, u32[]{:S(2)}) collective-permute-start(f32[24,640]{1,0:T(8,128)S(1)} %bitcast_add_fusion.9), channel_id=1, source_target_pairs={{0,960},{32,992},{64,0},{96,32},{128,64},{160,96},{192,128},{224,1... | collective-permute-start | bytes 184328 | tf_op jit(solution)/shard_map/ppermute | solution.py:92
  238.2 2.9 slice_select_fusion
  242.0 4.1 collective-permute-start.24
  248.6 5.4 %collective-permute-start.25 = (f32[24,640]{1,0:T(8,128)S(1)}, f32[24,640]{1,0:T(8,128)S(1)}, u32[]{:S(2)}, u32[]{:S(2)}) collective-permute-start(f32[24,640]{1,0:T(8,128)S(1)} %bitcast_add_fusion.7), channel_id=1, source_target_pairs={{0,960},{32,992},{64,0},{96,32},{128,64},{160,96},{192,128},{224,1... | collective-permute-start | bytes 184328 | tf_op jit(solution)/shard_map/ppermute | solution.py:92
  256.2 5.8 %collective-permute-start.26 = (f32[24,640]{1,0:T(8,128)S(1)}, f32[24,640]{1,0:T(8,128)S(1)}, u32[]{:S(2)}, u32[]{:S(2)}) collective-permute-start(f32[24,640]{1,0:T(8,128)S(1)} %bitcast_add_fusion.6), channel_id=1, source_target_pairs={{0,960},{32,992},{64,0},{96,32},{128,64},{160,96},{192,128},{224,1... | collective-permute-start | bytes 184328 | tf_op jit(solution)/shard_map/ppermute | solution.py:92
  264.2 5.8 %collective-permute-start.27 = (f32[24,640]{1,0:T(8,128)S(1)}, f32[24,640]{1,0:T(8,128)S(1)}, u32[]{:S(2)}, u32[]{:S(2)}) collective-permute-start(f32[24,640]{1,0:T(8,128)S(1)} %bitcast_add_fusion.5), channel_id=1, source_target_pairs={{0,960},{32,992},{64,0},{96,32},{128,64},{160,96},{192,128},{224,1... | collective-permute-start | bytes 184328 | tf_op jit(solution)/shard_map/ppermute | solution.py:92
  270.0 2.8 collective-permute-done.27
  273.6 6.0 %collective-permute-start.28 = (f32[24,640]{1,0:T(8,128)S(1)}, f32[24,640]{1,0:T(8,128)S(1)}, u32[]{:S(2)}, u32[]{:S(2)}) collective-permute-start(f32[24,640]{1,0:T(8,128)S(1)} %bitcast_add_fusion.4), channel_id=1, source_target_pairs={{0,960},{32,992},{64,0},{96,32},{128,64},{160,96},{192,128},{224,1... | collective-permute-start | bytes 184328 | tf_op jit(solution)/shard_map/ppermute | solution.py:92
  279.7 2.6 convolution_convert_fusion.1
  282.3 44.3 %collective-permute-start.32 = (bf16[1664,256]{1,0:T(8,128)(2,1)}, bf16[1664,256]{1,0:T(8,128)(2,1)}, u32[]{:S(2)}, u32[]{:S(2)}) collective-permute-start(bf16[1664,256]{1,0:T(8,128)(2,1)} %convolution_convert_fusion.1), channel_id=1, source_target_pairs={{0,32},{32,0},{64,96},{96,64},{128,160},{160,128},{192,224},{224,1... | collective-permute-start | bytes 2555912 | tf_op jit(solution)/shard_map/ppermute | solution.py:95
  327.5 1.9 collective-permute-start.29
  329.4 4.3 collective-permute-done.29
  334.6 3.9 collective-permute-start.30
  340.1 17.7 %collective-permute-start.33 = (bf16[256,1664]{1,0:T(8,128)(2,1)}, bf16[256,1664]{1,0:T(8,128)(2,1)}, u32[]{:S(2)}, u32[]{:S(2)}) collective-permute-start(bf16[256,1664]{1,0:T(8,128)(2,1)} %convolution_convert_fusion), channel_id=1, source_target_pairs={{0,32},{32,0},{64,96},{96,64},{128,160},{160,128},{192,224},{224,1... | collective-permute-start | bytes 2555912 | tf_op jit(solution)/shard_map/ppermute | solution.py:96
  358.7 2.9 collective-permute-start.31
  361.6 2.8 fusion.8
  366.0 22.3 %reduce-scatter.2.cloned.1.call-done = f32[1,24,1024]{2,1,0:T(8,128)} async-done(((f32[16,24,1024]{2,1,0:T(8,128)}), f32[1,24,1024]{2,1,0:T(8,128)}) %reduce-scatter.2.cloned.1.call-update) | async-done | bytes 98320 | tf_op jit(solution)/shard_map/reduce_scatter | solution.py:89
  390.9 32.0 %all-to-all-start.1 = ((bf16[32,2,624]{2,1,0:T(2,128)(2,1)}), bf16[32,2,624]{2,1,0:T(2,128)(2,1)S(1)}, u32[]{:S(2)}, u32[]{:S(2)}) async-start(bf16[32,2,624]{2,1,0:T(2,128)(2,1)} %reshape.132), calls=%async_computation.2 | async-start | bytes 163840 | tf_op jit(solution)/shard_map/all_to_all | solution.py:105
  422.9 2.8 fusion.9
  425.7 4.6 %all-to-all-done.1 = bf16[32,2,624]{2,1,0:T(2,128)(2,1)S(1)} async-done(((bf16[32,2,624]{2,1,0:T(2,128)(2,1)}), bf16[32,2,624]{2,1,0:T(2,128)(2,1)S(1)}, u32[]{:S(2)}, u32[]{:S(2)}) %all-to-all-start.1) | async-done | bytes 79904 | tf_op jit(solution)/shard_map/all_to_all | solution.py:105
  (115 shorter events, 37.9 us)
Async XLA Ops:
  7.2 25.9 %copy-start.6 = (bf16[320,2]{0,1:T(2,128)(2,1)S(1)}, bf16[320,2]{0,1:T(2,128)(2,1)}, u32[]{:S(2)}) copy-start(bf16[320,2]{0,1:T(2,128)(2,1)} %param.10) | copy-start | bytes 3844
  10.0 26.1 %all-to-all-start = ((bf16[32,24,104]{2,1,0:T(8,128)(2,1)}), bf16[32,24,104]{2,1,0:T(8,128)(2,1)S(1)}, u32[]{:S(2)}, u32[]{:S(2)}) async-start(bf16[32,24,104]{2,1,0:T(8,128)(2,1)} %bitcast), calls=%async_computation | async-start | bytes 393216 | tf_op jit(solution)/shard_map/all_to_all | solution.py:51
  27.7 144.4 %all-gather.2.cloned.1.call-start = ((), (), s32[]{:S(2)}) async-start(), calls=%async_computation.3 | async-start | bytes 1357824 | tf_op jit(solution)/shard_map/all_gather | solution.py:61
  27.7 147.6 %collective-permute-start.15 = (bf16[1664,256]{1,0:T(8,128)(2,1)}, bf16[1664,256]{1,0:T(8,128)(2,1)}, u32[]{:S(2)}, u32[]{:S(2)}) collective-permute-start(bf16[1664,256]{1,0:T(8,128)(2,1)} %bitcast.3), channel_id=1, source_target_pairs={{0,32},{32,0},{64,96},{96,64},{128,160},{160,128},{192,224},{224,1... | collective-permute-start | bytes 2555912 | tf_op jit(solution)/shard_map/ppermute | solution.py:39
  29.7 151.3 %collective-permute-start.16 = (bf16[256,1664]{1,0:T(8,128)(2,1)}, bf16[256,1664]{1,0:T(8,128)(2,1)}, u32[]{:S(2)}, u32[]{:S(2)}) collective-permute-start(bf16[256,1664]{1,0:T(8,128)(2,1)} %bitcast.20), channel_id=1, source_target_pairs={{0,32},{32,0},{64,96},{96,64},{128,160},{160,128},{192,224},{224,1... | collective-permute-start | bytes 2555912 | tf_op jit(solution)/shard_map/ppermute | solution.py:40
  36.9 11.3 %collective-permute-start = (bf16[24,1664]{1,0:T(8,128)(2,1)S(1)}, bf16[24,1664]{1,0:T(8,128)(2,1)S(1)}, u32[]{:S(2)}, u32[]{:S(2)}) collective-permute-start(bf16[24,1664]{1,0:T(8,128)(2,1)S(1)} %squeeze.68), channel_id=1, source_target_pairs={{0,960},{32,992},{64,0},{96,32},{128,64},{160,96},{192,128},{224,1... | collective-permute-start | bytes 239624 | tf_op jit(solution)/shard_map/ppermute | solution.py:67
  47.6 340.7 %reduce-scatter.2.cloned.1.call-start = ((), (), s32[]{:S(2)}) async-start(), calls=%async_computation.4 | async-start | bytes 1671168 | tf_op jit(solution)/shard_map/reduce_scatter | solution.py:89
  48.2 7.7 %collective-permute-start.1 = (bf16[24,1664]{1,0:T(8,128)(2,1)S(1)}, bf16[24,1664]{1,0:T(8,128)(2,1)S(1)}, u32[]{:S(2)}, u32[]{:S(2)}) collective-permute-start(bf16[24,1664]{1,0:T(8,128)(2,1)S(1)} %collective-permute-done), channel_id=1, source_target_pairs={{0,960},{32,992},{64,0},{96,32},{128,64},{160,96},{192,128},{224,1... | collective-permute-start | bytes 239624 | tf_op jit(solution)/shard_map/ppermute | solution.py:67
  55.9 7.4 %collective-permute-start.2 = (bf16[24,1664]{1,0:T(8,128)(2,1)S(1)}, bf16[24,1664]{1,0:T(8,128)(2,1)S(1)}, u32[]{:S(2)}, u32[]{:S(2)}) collective-permute-start(bf16[24,1664]{1,0:T(8,128)(2,1)S(1)} %collective-permute-done.1), channel_id=1, source_target_pairs={{0,960},{32,992},{64,0},{96,32},{128,64},{160,96},{192,128},{224,1... | collective-permute-start | bytes 239624 | tf_op jit(solution)/shard_map/ppermute | solution.py:67
  63.3 7.8 %collective-permute-start.3 = (bf16[24,1664]{1,0:T(8,128)(2,1)S(1)}, bf16[24,1664]{1,0:T(8,128)(2,1)S(1)}, u32[]{:S(2)}, u32[]{:S(2)}) collective-permute-start(bf16[24,1664]{1,0:T(8,128)(2,1)S(1)} %collective-permute-done.2), channel_id=1, source_target_pairs={{0,960},{32,992},{64,0},{96,32},{128,64},{160,96},{192,128},{224,1... | collective-permute-start | bytes 239624 | tf_op jit(solution)/shard_map/ppermute | solution.py:67
  71.1 7.9 %collective-permute-start.4 = (bf16[24,1664]{1,0:T(8,128)(2,1)S(1)}, bf16[24,1664]{1,0:T(8,128)(2,1)S(1)}, u32[]{:S(2)}, u32[]{:S(2)}) collective-permute-start(bf16[24,1664]{1,0:T(8,128)(2,1)S(1)} %collective-permute-done.3), channel_id=1, source_target_pairs={{0,960},{32,992},{64,0},{96,32},{128,64},{160,96},{192,128},{224,1... | collective-permute-start | bytes 239624 | tf_op jit(solution)/shard_map/ppermute | solution.py:67
  79.0 9.0 %collective-permute-start.5 = (bf16[24,1664]{1,0:T(8,128)(2,1)S(1)}, bf16[24,1664]{1,0:T(8,128)(2,1)S(1)}, u32[]{:S(2)}, u32[]{:S(2)}) collective-permute-start(bf16[24,1664]{1,0:T(8,128)(2,1)S(1)} %collective-permute-done.4), channel_id=1, source_target_pairs={{0,960},{32,992},{64,0},{96,32},{128,64},{160,96},{192,128},{224,1... | collective-permute-start | bytes 239624 | tf_op jit(solution)/shard_map/ppermute | solution.py:67
  87.9 8.6 %collective-permute-start.6 = (bf16[24,1664]{1,0:T(8,128)(2,1)S(1)}, bf16[24,1664]{1,0:T(8,128)(2,1)S(1)}, u32[]{:S(2)}, u32[]{:S(2)}) collective-permute-start(bf16[24,1664]{1,0:T(8,128)(2,1)S(1)} %collective-permute-done.5), channel_id=1, source_target_pairs={{0,960},{32,992},{64,0},{96,32},{128,64},{160,96},{192,128},{224,1... | collective-permute-start | bytes 239624 | tf_op jit(solution)/shard_map/ppermute | solution.py:67
  96.5 9.4 %collective-permute-start.7 = (bf16[24,1664]{1,0:T(8,128)(2,1)S(1)}, bf16[24,1664]{1,0:T(8,128)(2,1)S(1)}, u32[]{:S(2)}, u32[]{:S(2)}) collective-permute-start(bf16[24,1664]{1,0:T(8,128)(2,1)S(1)} %collective-permute-done.6), channel_id=1, source_target_pairs={{0,960},{32,992},{64,0},{96,32},{128,64},{160,96},{192,128},{224,1... | collective-permute-start | bytes 239624 | tf_op jit(solution)/shard_map/ppermute | solution.py:67
  105.9 10.8 %collective-permute-start.8 = (bf16[24,1664]{1,0:T(8,128)(2,1)S(1)}, bf16[24,1664]{1,0:T(8,128)(2,1)S(1)}, u32[]{:S(2)}, u32[]{:S(2)}) collective-permute-start(bf16[24,1664]{1,0:T(8,128)(2,1)S(1)} %collective-permute-done.7), channel_id=1, source_target_pairs={{0,960},{32,992},{64,0},{96,32},{128,64},{160,96},{192,128},{224,1... | collective-permute-start | bytes 239624 | tf_op jit(solution)/shard_map/ppermute | solution.py:67
  116.7 10.4 %collective-permute-start.9 = (bf16[24,1664]{1,0:T(8,128)(2,1)S(1)}, bf16[24,1664]{1,0:T(8,128)(2,1)S(1)}, u32[]{:S(2)}, u32[]{:S(2)}) collective-permute-start(bf16[24,1664]{1,0:T(8,128)(2,1)S(1)} %collective-permute-done.8), channel_id=1, source_target_pairs={{0,960},{32,992},{64,0},{96,32},{128,64},{160,96},{192,128},{224,1... | collective-permute-start | bytes 239624 | tf_op jit(solution)/shard_map/ppermute | solution.py:67
  127.1 9.6 %collective-permute-start.10 = (bf16[24,1664]{1,0:T(8,128)(2,1)S(1)}, bf16[24,1664]{1,0:T(8,128)(2,1)S(1)}, u32[]{:S(2)}, u32[]{:S(2)}) collective-permute-start(bf16[24,1664]{1,0:T(8,128)(2,1)S(1)} %collective-permute-done.9), channel_id=1, source_target_pairs={{0,960},{32,992},{64,0},{96,32},{128,64},{160,96},{192,128},{224,1... | collective-permute-start | bytes 239624 | tf_op jit(solution)/shard_map/ppermute | solution.py:67
  136.7 9.3 %collective-permute-start.11 = (bf16[24,1664]{1,0:T(8,128)(2,1)S(1)}, bf16[24,1664]{1,0:T(8,128)(2,1)S(1)}, u32[]{:S(2)}, u32[]{:S(2)}) collective-permute-start(bf16[24,1664]{1,0:T(8,128)(2,1)S(1)} %collective-permute-done.10), channel_id=1, source_target_pairs={{0,960},{32,992},{64,0},{96,32},{128,64},{160,96},{192,128},{224,1... | collective-permute-start | bytes 239624 | tf_op jit(solution)/shard_map/ppermute | solution.py:67
  145.9 8.7 %collective-permute-start.12 = (bf16[24,1664]{1,0:T(8,128)(2,1)S(1)}, bf16[24,1664]{1,0:T(8,128)(2,1)S(1)}, u32[]{:S(2)}, u32[]{:S(2)}) collective-permute-start(bf16[24,1664]{1,0:T(8,128)(2,1)S(1)} %collective-permute-done.11), channel_id=1, source_target_pairs={{0,960},{32,992},{64,0},{96,32},{128,64},{160,96},{192,128},{224,1... | collective-permute-start | bytes 239624 | tf_op jit(solution)/shard_map/ppermute | solution.py:67
  154.6 8.7 %collective-permute-start.13 = (bf16[24,1664]{1,0:T(8,128)(2,1)S(1)}, bf16[24,1664]{1,0:T(8,128)(2,1)S(1)}, u32[]{:S(2)}, u32[]{:S(2)}) collective-permute-start(bf16[24,1664]{1,0:T(8,128)(2,1)S(1)} %collective-permute-done.12), channel_id=1, source_target_pairs={{0,960},{32,992},{64,0},{96,32},{128,64},{160,96},{192,128},{224,1... | collective-permute-start | bytes 239624 | tf_op jit(solution)/shard_map/ppermute | solution.py:67
  163.3 8.7 %collective-permute-start.14 = (bf16[24,1664]{1,0:T(8,128)(2,1)S(1)}, bf16[24,1664]{1,0:T(8,128)(2,1)S(1)}, u32[]{:S(2)}, u32[]{:S(2)}) collective-permute-start(bf16[24,1664]{1,0:T(8,128)(2,1)S(1)} %collective-permute-done.13), channel_id=1, source_target_pairs={{0,960},{32,992},{64,0},{96,32},{128,64},{160,96},{192,128},{224,1... | collective-permute-start | bytes 239624 | tf_op jit(solution)/shard_map/ppermute | solution.py:67
  172.9 2.5 copy-start
  179.0 2.0 copy-start.3
  182.8 2.0 copy-start.5
  184.8 23.4 %copy-start.1 = (f32[384,1664]{1,0:T(8,128)}, f32[384,1664]{1,0:T(8,128)S(1)}, u32[]{:S(2)}) copy-start(f32[384,1664]{1,0:T(8,128)S(1)} %convolution_add_fusion) | copy-start | bytes 7667716
  184.9 38.7 %copy-start.2 = (f32[16,24,640]{2,1,0:T(8,128)}, f32[16,24,640]{2,1,0:T(8,128)S(1)}, u32[]{:S(2)}) copy-start(f32[16,24,640]{2,1,0:T(8,128)S(1)} %slice.56) | copy-start | bytes 2949124
  185.0 8.0 %collective-permute-start.17 = (f32[24,640]{1,0:T(8,128)S(1)}, f32[24,640]{1,0:T(8,128)S(1)}, u32[]{:S(2)}, u32[]{:S(2)}) collective-permute-start(f32[24,640]{1,0:T(8,128)S(1)} %dynamic-slice_bitcast_fusion), channel_id=1, source_target_pairs={{0,960},{32,992},{64,0},{96,32},{128,64},{160,96},{192,128},{224,1... | collective-permute-start | bytes 184328 | tf_op jit(solution)/shard_map/ppermute | solution.py:92
  193.0 7.3 %collective-permute-start.18 = (f32[24,640]{1,0:T(8,128)S(1)}, f32[24,640]{1,0:T(8,128)S(1)}, u32[]{:S(2)}, u32[]{:S(2)}) collective-permute-start(f32[24,640]{1,0:T(8,128)S(1)} %bitcast_add_fusion.14), channel_id=1, source_target_pairs={{0,960},{32,992},{64,0},{96,32},{128,64},{160,96},{192,128},{224,1... | collective-permute-start | bytes 184328 | tf_op jit(solution)/shard_map/ppermute | solution.py:92
  200.3 7.9 %collective-permute-start.19 = (f32[24,640]{1,0:T(8,128)S(1)}, f32[24,640]{1,0:T(8,128)S(1)}, u32[]{:S(2)}, u32[]{:S(2)}) collective-permute-start(f32[24,640]{1,0:T(8,128)S(1)} %bitcast_add_fusion.13), channel_id=1, source_target_pairs={{0,960},{32,992},{64,0},{96,32},{128,64},{160,96},{192,128},{224,1... | collective-permute-start | bytes 184328 | tf_op jit(solution)/shard_map/ppermute | solution.py:92
  208.3 8.1 %collective-permute-start.20 = (f32[24,640]{1,0:T(8,128)S(1)}, f32[24,640]{1,0:T(8,128)S(1)}, u32[]{:S(2)}, u32[]{:S(2)}) collective-permute-start(f32[24,640]{1,0:T(8,128)S(1)} %bitcast_add_fusion.12), channel_id=1, source_target_pairs={{0,960},{32,992},{64,0},{96,32},{128,64},{160,96},{192,128},{224,1... | collective-permute-start | bytes 184328 | tf_op jit(solution)/shard_map/ppermute | solution.py:92
  216.4 7.2 %collective-permute-start.21 = (f32[24,640]{1,0:T(8,128)S(1)}, f32[24,640]{1,0:T(8,128)S(1)}, u32[]{:S(2)}, u32[]{:S(2)}) collective-permute-start(f32[24,640]{1,0:T(8,128)S(1)} %bitcast_add_fusion.11), channel_id=1, source_target_pairs={{0,960},{32,992},{64,0},{96,32},{128,64},{160,96},{192,128},{224,1... | collective-permute-start | bytes 184328 | tf_op jit(solution)/shard_map/ppermute | solution.py:92
  223.6 7.9 %collective-permute-start.22 = (f32[24,640]{1,0:T(8,128)S(1)}, f32[24,640]{1,0:T(8,128)S(1)}, u32[]{:S(2)}, u32[]{:S(2)}) collective-permute-start(f32[24,640]{1,0:T(8,128)S(1)} %bitcast_add_fusion.10), channel_id=1, source_target_pairs={{0,960},{32,992},{64,0},{96,32},{128,64},{160,96},{192,128},{224,1... | collective-permute-start | bytes 184328 | tf_op jit(solution)/shard_map/ppermute | solution.py:92
  232.4 8.7 %collective-permute-start.23 = (f32[24,640]{1,0:T(8,128)S(1)}, f32[24,640]{1,0:T(8,128)S(1)}, u32[]{:S(2)}, u32[]{:S(2)}) collective-permute-start(f32[24,640]{1,0:T(8,128)S(1)} %bitcast_add_fusion.9), channel_id=1, source_target_pairs={{0,960},{32,992},{64,0},{96,32},{128,64},{160,96},{192,128},{224,1... | collective-permute-start | bytes 184328 | tf_op jit(solution)/shard_map/ppermute | solution.py:92
  242.0 5.9 %collective-permute-start.24 = (f32[24,640]{1,0:T(8,128)S(1)}, f32[24,640]{1,0:T(8,128)S(1)}, u32[]{:S(2)}, u32[]{:S(2)}) collective-permute-start(f32[24,640]{1,0:T(8,128)S(1)} %bitcast_add_fusion.8), channel_id=1, source_target_pairs={{0,960},{32,992},{64,0},{96,32},{128,64},{160,96},{192,128},{224,1... | collective-permute-start | bytes 184328 | tf_op jit(solution)/shard_map/ppermute | solution.py:92
  248.6 6.7 %collective-permute-start.25 = (f32[24,640]{1,0:T(8,128)S(1)}, f32[24,640]{1,0:T(8,128)S(1)}, u32[]{:S(2)}, u32[]{:S(2)}) collective-permute-start(f32[24,640]{1,0:T(8,128)S(1)} %bitcast_add_fusion.7), channel_id=1, source_target_pairs={{0,960},{32,992},{64,0},{96,32},{128,64},{160,96},{192,128},{224,1... | collective-permute-start | bytes 184328 | tf_op jit(solution)/shard_map/ppermute | solution.py:92
  256.2 7.1 %collective-permute-start.26 = (f32[24,640]{1,0:T(8,128)S(1)}, f32[24,640]{1,0:T(8,128)S(1)}, u32[]{:S(2)}, u32[]{:S(2)}) collective-permute-start(f32[24,640]{1,0:T(8,128)S(1)} %bitcast_add_fusion.6), channel_id=1, source_target_pairs={{0,960},{32,992},{64,0},{96,32},{128,64},{160,96},{192,128},{224,1... | collective-permute-start | bytes 184328 | tf_op jit(solution)/shard_map/ppermute | solution.py:92
  264.2 8.6 %collective-permute-start.27 = (f32[24,640]{1,0:T(8,128)S(1)}, f32[24,640]{1,0:T(8,128)S(1)}, u32[]{:S(2)}, u32[]{:S(2)}) collective-permute-start(f32[24,640]{1,0:T(8,128)S(1)} %bitcast_add_fusion.5), channel_id=1, source_target_pairs={{0,960},{32,992},{64,0},{96,32},{128,64},{160,96},{192,128},{224,1... | collective-permute-start | bytes 184328 | tf_op jit(solution)/shard_map/ppermute | solution.py:92
  273.6 53.0 %collective-permute-start.28 = (f32[24,640]{1,0:T(8,128)S(1)}, f32[24,640]{1,0:T(8,128)S(1)}, u32[]{:S(2)}, u32[]{:S(2)}) collective-permute-start(f32[24,640]{1,0:T(8,128)S(1)} %bitcast_add_fusion.4), channel_id=1, source_target_pairs={{0,960},{32,992},{64,0},{96,32},{128,64},{160,96},{192,128},{224,1... | collective-permute-start | bytes 184328 | tf_op jit(solution)/shard_map/ppermute | solution.py:92
  282.3 79.3 %collective-permute-start.32 = (bf16[1664,256]{1,0:T(8,128)(2,1)}, bf16[1664,256]{1,0:T(8,128)(2,1)}, u32[]{:S(2)}, u32[]{:S(2)}) collective-permute-start(bf16[1664,256]{1,0:T(8,128)(2,1)} %convolution_convert_fusion.1), channel_id=1, source_target_pairs={{0,32},{32,0},{64,96},{96,64},{128,160},{160,128},{192,224},{224,1... | collective-permute-start | bytes 2555912 | tf_op jit(solution)/shard_map/ppermute | solution.py:95
  327.5 6.3 %collective-permute-start.29 = (f32[24,640]{1,0:T(8,128)S(1)}, f32[24,640]{1,0:T(8,128)S(1)}, u32[]{:S(2)}, u32[]{:S(2)}) collective-permute-start(f32[24,640]{1,0:T(8,128)S(1)} %bitcast_add_fusion.3), channel_id=1, source_target_pairs={{0,960},{32,992},{64,0},{96,32},{128,64},{160,96},{192,128},{224,1... | collective-permute-start | bytes 184328 | tf_op jit(solution)/shard_map/ppermute | solution.py:92
  334.6 27.0 %copy-start.4 = (f32[384,256]{0,1:T(8,128)S(1)}, f32[384,256]{0,1:T(8,128)}, u32[]{:S(2)}) copy-start(f32[384,256]{0,1:T(8,128)} %copy-done.3) | copy-start | bytes 1179652
  334.6 23.2 %collective-permute-start.30 = (f32[24,640]{1,0:T(8,128)S(1)}, f32[24,640]{1,0:T(8,128)S(1)}, u32[]{:S(2)}, u32[]{:S(2)}) collective-permute-start(f32[24,640]{1,0:T(8,128)S(1)} %bitcast_add_fusion.2), channel_id=1, source_target_pairs={{0,960},{32,992},{64,0},{96,32},{128,64},{160,96},{192,128},{224,1... | collective-permute-start | bytes 184328 | tf_op jit(solution)/shard_map/ppermute | solution.py:92
  340.1 82.8 %collective-permute-start.33 = (bf16[256,1664]{1,0:T(8,128)(2,1)}, bf16[256,1664]{1,0:T(8,128)(2,1)}, u32[]{:S(2)}, u32[]{:S(2)}) collective-permute-start(bf16[256,1664]{1,0:T(8,128)(2,1)} %convolution_convert_fusion), channel_id=1, source_target_pairs={{0,32},{32,0},{64,96},{96,64},{128,160},{160,128},{192,224},{224,1... | collective-permute-start | bytes 2555912 | tf_op jit(solution)/shard_map/ppermute | solution.py:96
  358.7 6.5 %collective-permute-start.31 = (f32[24,640]{1,0:T(8,128)S(1)}, f32[24,640]{1,0:T(8,128)S(1)}, u32[]{:S(2)}, u32[]{:S(2)}) collective-permute-start(f32[24,640]{1,0:T(8,128)S(1)} %bitcast_add_fusion.1), channel_id=1, source_target_pairs={{0,960},{32,992},{64,0},{96,32},{128,64},{160,96},{192,128},{224,1... | collective-permute-start | bytes 184328 | tf_op jit(solution)/shard_map/ppermute | solution.py:92
  390.9 39.4 %all-to-all-start.1 = ((bf16[32,2,624]{2,1,0:T(2,128)(2,1)}), bf16[32,2,624]{2,1,0:T(2,128)(2,1)S(1)}, u32[]{:S(2)}, u32[]{:S(2)}) async-start(bf16[32,2,624]{2,1,0:T(2,128)(2,1)} %reshape.132), calls=%async_computation.2 | async-start | bytes 163840 | tf_op jit(solution)/shard_map/all_to_all | solution.py:105
Sparse Core Ops, SparseCore 0:
  47.7 82.5 all-gather.1
  241.2 147.0 reduce-scatter.1

commit v2 on v1

v2 whole, which is shorter than its diff:
```python
import math

import jax
import jax.numpy as jnp
from jax import lax
from jax.sharding import PartitionSpec as P

BF16 = jnp.bfloat16
F32 = jnp.float32


def gelu_pair(values):
    cumul = 0.5 * (1.0 + lax.erf(values * (1.0 / math.sqrt(2.0))))
    density = jnp.exp(-0.5 * values * values) * (1.0 / math.sqrt(2.0 * math.pi))
    return values * cumul, cumul + values * density


def dot(left, right, dims):
    return lax.dot_general(left, right, ((dims[0], dims[1]), ((), ())), preferred_element_type=F32)


def pieces(values, cuts):
    sizes = [values.shape[0] // cuts // 16 * 16] * (cuts - 1)
    sizes.append(values.shape[0] - sum(sizes))
    starts = [sum(sizes[:i]) for i in range(cuts)]
    return [values[at:at + size] for at, size in zip(starts, sizes)]


def body(tokens, cotangent, gate_values, route_ids, route_slots, kept_mask, weight_in, weight_out):
    experts = lax.axis_size("expert")
    dp = lax.axis_size("dp")
    ring = dp // 2
    half = ring // 2
    tok_rows, piece = tokens.shape
    width = piece * experts
    top = route_ids.shape[1]
    cap = (21 * top * tok_rows + 20 * experts - 1) // (20 * experts)
    pad = (cap + 1 + 7) // 8 * 8
    me = lax.axis_index("expert")

    def shift(values, by):
        return lax.ppermute(values, "dp", [(i, (i + by) % dp) for i in range(dp)])

    def swap(values):
        return lax.ppermute(values, "dp", [(i, i ^ 1) for i in range(dp)])

    own_in, own_out = weight_in[0], weight_out[0]
    mate_out = swap(own_out)

    kept = kept_mask == 1
    target = jnp.where(kept, route_ids * pad + route_slots, -1)
    slots = jnp.arange(experts * pad, dtype=jnp.int32)
    both = jnp.concatenate([tokens, cotangent], axis=1)
    spread = jnp.zeros((experts * pad, tok_rows), jnp.bool_)
    for k in range(top):
        spread = spread | (slots[:, None] == target[None, :, k])
    placed = dot(spread.astype(BF16), both, ((1,), (0,))).astype(BF16)
    placed = placed.reshape(experts, pad, 2 * piece)
    arrived = lax.all_to_all(placed, "expert", split_axis=0, concat_axis=0, tiled=True)
    arrived = arrived.reshape(experts, pad, 2, piece).transpose(1, 2, 0, 3).reshape(pad, 2 * width)

    own_slots = jnp.arange(2 * width, dtype=jnp.int32)
    hit = (target[:, :, None] == me * pad + own_slots[None, None, :]) & (own_slots < cap)[None, None, :]
    own_gates = jnp.sum(jnp.where(hit, gate_values.astype(F32)[:, :, None], 0.0), axis=(0, 1))
    spare = lax.broadcasted_iota(jnp.int32, (pad, 2 * width), 0) == cap
    block = jnp.where(spare, own_gates.astype(BF16)[None, :], arrived)

    found = {0: block}
    ahead = behind = block
    queue, mate_in = pieces(own_in, 4), []
    for step in range(half):
        sent = [queue.pop(0)] if queue and step > 0 else []
        ahead, behind, *sent = lax.optimization_barrier((ahead, behind, *sent))
        ahead = shift(ahead, 2)
        found[-step - 1] = ahead
        if step + 1 < ring - half:
            behind = shift(behind, -2)
            found[step + 1] = behind
        if sent:
            got = swap(sent[0])
            ahead, behind, got = lax.optimization_barrier((ahead, behind, got))
            mate_in.append(got)
    while queue:
        mate_in.append(swap(queue.pop(0)))
    mate_in = jnp.concatenate(mate_in, axis=0)
    order = sorted(found)
    gathered = jnp.stack([found[at] for at in order])
    gates = jnp.pad(gathered[:, cap, :cap].astype(F32), ((0, 0), (0, pad - cap))).reshape(ring * pad, 1)
    gathered = gathered.reshape(ring * pad, 2 * width)
    rows, grads = gathered[:, :width], gathered[:, width:]

    gate_terms = jnp.zeros((ring * pad,), F32)
    slopes, lows = [], []
    for first, second in ((own_in, own_out), (mate_in, mate_out)):
        pre = dot(rows, first, ((1,), (0,)))
        raw = dot(grads, second, ((1,), (1,)))
        hidden, slope = gelu_pair(pre)
        gate_terms = gate_terms + jnp.sum(hidden * raw, axis=1)
        slopes.append((gates * raw * slope).astype(BF16))
        lows.append(hidden.astype(BF16))
    row_terms = dot(slopes[0], own_in, ((1,), (1,))) + dot(slopes[1], mate_in, ((1,), (1,)))
    row_terms = row_terms.reshape(ring, pad, width)
    gate_terms = jnp.pad(gate_terms.reshape(ring, pad)[:, :cap], ((0, 0), (0, width - cap)))
    spare_row = lax.broadcasted_iota(jnp.int32, (1, pad, 1), 1) == cap
    terms = jnp.where(spare_row, gate_terms[:, None, :], row_terms)
    part = {at: terms[i] for i, at in enumerate(order)}

    scaled = (gates * grads.astype(F32)).astype(BF16)
    queue = pieces(dot(rows, slopes[1], ((0,), (0,))).astype(BF16), 4)
    queue += pieces(dot(lows[1], scaled, ((0,), (0,))).astype(BF16), 3)
    swapped = []
    plus, minus = part[-half], part[ring - half - 1]
    for step in range(half):
        sent = [queue.pop(0)] if queue and step > 0 else []
        plus, minus, *sent = lax.optimization_barrier((plus, minus, *sent))
        at = half - 1 - step
        plus = shift(plus, -2)
        if step > 0:
            minus = shift(minus, 2)
        if sent:
            got = swap(sent[0])
            plus, minus, got = lax.optimization_barrier((plus, minus, got))
            swapped.append(got)
        if at > 0:
            plus = plus + part[-at]
        if step > 0 and at > 0:
            minus = minus + part[at]
    summed = plus + minus + part[0]
    while queue:
        swapped.append(swap(queue.pop(0)))
    mate_first = jnp.concatenate(swapped[:4], axis=0)
    mate_second = jnp.concatenate(swapped[4:], axis=0)
    grad_first = (dot(rows, slopes[0], ((0,), (0,))) + mate_first.astype(F32)).astype(BF16)
    grad_second = (dot(lows[0], scaled, ((0,), (0,))) + mate_second.astype(F32)).astype(BF16)

    slot_gates = jnp.pad(summed[cap, :cap].astype(BF16), (0, piece - cap))
    grad_rows = summed.astype(BF16).reshape(pad, experts, piece).transpose(1, 0, 2)
    spare_slot = lax.broadcasted_iota(jnp.int32, (1, pad, 1), 1) == cap
    grad_rows = jnp.where(spare_slot, slot_gates[None, None, :], grad_rows)
    returned = lax.all_to_all(grad_rows, "expert", split_axis=0, concat_axis=0, tiled=True)
    gates_back = jnp.pad(returned[:, cap, :cap], ((0, 0), (0, pad - cap))).reshape(experts * pad)
    returned = returned.reshape(experts * pad, piece)
    gather = jnp.zeros((tok_rows, experts * pad), jnp.bool_)
    gate_out = []
    for k in range(top):
        match = target[:, k, None] == slots[None, :]
        gather = gather | match
        gate_out.append(jnp.sum(jnp.where(match, gates_back.astype(F32)[None, :], 0.0), axis=1))
    token_grads = dot(gather.astype(BF16), returned, ((1,), (0,))).astype(BF16)
    return token_grads, jnp.stack(gate_out, axis=1), grad_first[None], grad_second[None]


def solution(mesh):
    return jax.shard_map(
        body,
        mesh=mesh,
        in_specs=(
            P("dp", "expert"),
            P("dp", "expert"),
            P("dp", None),
            P("dp", None),
            P("dp", None),
            P("dp", None),
            P("expert", None, "dp"),
            P("expert", "dp", None),
        ),
        out_specs=(
            P("dp", "expert"),
            P("dp", None),
            P("expert", None, "dp"),
            P("expert", "dp", None),
        ),
        check_vma=False,
    )
```

time: 444 us -> 337 us (0.76)
  starting transfers between devices: 293 us -> 201 us
  waiting for transfers between devices: 86.4 us -> 104 us
  between operations: 15.2 us -> 1.84 us
  other arithmetic: 15.7 us -> 5.28 us
  matrix products: 23.9 us -> 15.8 us
    ppermute x34 -> x42, starting transfers between devices: 243 us -> 167 us  [the longest x30 127 us: shift(): return lax.ppermute(values, 'dp', [(i, (i + by) % dp) for i in range(dp)])]
    ppermute x34 -> x42, waiting for transfers between devices: 57.7 us -> 93.2 us  [the longest x30 77.7 us: shift(): return lax.ppermute(values, 'dp', [(i, (i + by) % dp) for i in range(dp)])]
    reduce_scatter x1 -> x0, waiting for transfers between devices: 22.3 us -> none  [body(): lax.psum_scatter(near, 'dp', scatter_dimension=0, axis_index_groups=groups)]
    all_to_all x1, starting transfers between devices: 32 us -> 16.3 us  [body(): lax.all_to_all(grad_rows, 'expert', split_axis=0, concat_axis=0, tiled=True)]
    dot_general x12, matrix products: 23.9 us -> 15.8 us  [dot(): lax.dot_general(left, right, ((dims[0], dims[1]), ((), ())), preferred_el...]
    add x14 -> x7, other arithmetic: 7.61 us -> 0.32 us  [the longest x6 0.3 us: body(): minus = minus + part[at]]
  transfers between devices with their start and end apart: 38 -> 44, of which waited for: 30 -> 28; matrix products, arithmetic and copies ran while one was open for 8% -> 4% of each run, Pallas kernels for 0% -> 0%
where the time goes in v2:
time: 337 us; the launch traced here: 335 us
  starting transfers between devices  201 us (60%)
  waiting for transfers between devices  104 us (31%)
  matrix products  15.8 us (5%)
  local copies, waits for them, and re-layouts  7.76 us (2%)
  other arithmetic  5.28 us (2%)
    ppermute x30, starting transfers between devices, shift(): return lax.ppermute(values, 'dp', [(i, (i + by) % dp) for i in range(dp)])  127 us
    ppermute x30, waiting for transfers between devices, shift(): return lax.ppermute(values, 'dp', [(i, (i + by) % dp) for i in range(dp)])  77.7 us
    ppermute x12, starting transfers between devices, swap(): return lax.ppermute(values, 'dp', [(i, i ^ 1) for i in range(dp)])  39.9 us
    all_to_all x1, starting transfers between devices, body(): lax.all_to_all(placed, 'expert', split_axis=0, concat_axis=0, tiled=True)  17.7 us
    all_to_all x1, starting transfers between devices, body(): lax.all_to_all(grad_rows, 'expert', split_axis=0, concat_axis=0, tiled=True)  16.3 us
    dot_general x12, matrix products, dot(): lax.dot_general(left, right, ((dims[0], dims[1]), ((), ())), preferred_el...  15.8 us
    ppermute x12, waiting for transfers between devices, swap(): return lax.ppermute(values, 'dp', [(i, i ^ 1) for i in range(dp)])  15.5 us
  transfers between devices with their start and end apart: 44, of which 28 were waited for; matrix products, arithmetic and copies ran while one was open for 4% of the time, Pallas kernels for 0%

profile of v2, /device:TPU:1, one launch (start us, length us, event | category | flops | bytes accessed | tf_op | source)
XLA Modules:
  0.0 335.3 jit_solution(2199893803025084147)
XLA Ops:
  3.5 17.7 %all-to-all-start = ((bf16[32,24,104]{2,1,0:T(8,128)(2,1)}), bf16[32,24,104]{2,1,0:T(8,128)(2,1)S(1)}, u32[]{:S(2)}, u32[]{:S(2)}) async-start(bf16[32,24,104]{2,1,0:T(8,128)(2,1)} %bitcast), calls=%async_computation | async-start | bytes 393216 | tf_op jit(solution)/shard_map/all_to_all | solution.py:59
  23.8 5.8 %all-to-all-done = bf16[32,24,104]{2,1,0:T(8,128)(2,1)S(1)} async-done(((bf16[32,24,104]{2,1,0:T(8,128)(2,1)}), bf16[32,24,104]{2,1,0:T(8,128)(2,1)S(1)}, u32[]{:S(2)}, u32[]{:S(2)}) %all-to-all-start) | async-done | bytes 159776 | tf_op jit(solution)/shard_map/all_to_all | solution.py:59
  30.6 1.9 collective-permute-start
  32.5 9.6 %collective-permute-start.1 = (bf16[24,3328]{1,0:T(8,128)(2,1)S(1)}, bf16[24,3328]{1,0:T(8,128)(2,1)S(1)}, u32[]{:S(2)}, u32[]{:S(2)}) collective-permute-start(bf16[24,3328]{1,0:T(8,128)(2,1)S(1)} %broadcast_select_fusion.1), channel_id=1, source_target_pairs={{0,960},{32,992},{64,0},{96,32},{128,64},{160,96},{192,128},{224,1... | collective-permute-start | bytes 479240 | tf_op jit(solution)/shard_map/ppermute | solution.py:42
  42.2 3.0 collective-permute-done
  45.2 3.8 %collective-permute-done.1 = bf16[24,3328]{1,0:T(8,128)(2,1)S(1)} collective-permute-done((bf16[24,3328]{1,0:T(8,128)(2,1)S(1)}, bf16[24,3328]{1,0:T(8,128)(2,1)S(1)}, u32[]{:S(2)}, u32[]{:S(2)}) %collective-permute-start.1) | collective-permute-done | bytes 159776 | tf_op jit(solution)/shard_map/ppermute | solution.py:42
  50.9 1.9 collective-permute-start.2
  52.8 6.2 %collective-permute-start.3 = (bf16[24,3328]{1,0:T(8,128)(2,1)S(1)}, bf16[24,3328]{1,0:T(8,128)(2,1)S(1)}, u32[]{:S(2)}, u32[]{:S(2)}) collective-permute-start(bf16[24,3328]{1,0:T(8,128)(2,1)S(1)} %collective-permute-done.1), channel_id=1, source_target_pairs={{0,960},{32,992},{64,0},{96,32},{128,64},{160,96},{192,128},{224,1... | collective-permute-start | bytes 479240 | tf_op jit(solution)/shard_map/ppermute | solution.py:42
  59.1 7.7 %collective-permute-done.2 = bf16[24,3328]{1,0:T(8,128)(2,1)S(1)} collective-permute-done((bf16[24,3328]{1,0:T(8,128)(2,1)S(1)}, bf16[24,3328]{1,0:T(8,128)(2,1)S(1)}, u32[]{:S(2)}, u32[]{:S(2)}) %collective-permute-start.2) | collective-permute-done | bytes 159776 | tf_op jit(solution)/shard_map/ppermute | solution.py:42
  66.8 1.9 collective-permute-start.7
  68.7 1.9 collective-permute-start.5
  70.6 5.5 %collective-permute-start.6 = (bf16[24,3328]{1,0:T(8,128)(2,1)S(1)}, bf16[24,3328]{1,0:T(8,128)(2,1)S(1)}, u32[]{:S(2)}, u32[]{:S(2)}) collective-permute-start(bf16[24,3328]{1,0:T(8,128)(2,1)S(1)} %collective-permute-done.3), channel_id=1, source_target_pairs={{0,960},{32,992},{64,0},{96,32},{128,64},{160,96},{192,128},{224,1... | collective-permute-start | bytes 479240 | tf_op jit(solution)/shard_map/ppermute | solution.py:42
  76.1 4.4 %collective-permute-done.5 = bf16[24,3328]{1,0:T(8,128)(2,1)S(1)} collective-permute-done((bf16[24,3328]{1,0:T(8,128)(2,1)S(1)}, bf16[24,3328]{1,0:T(8,128)(2,1)S(1)}, u32[]{:S(2)}, u32[]{:S(2)}) %collective-permute-start.5) | collective-permute-done | bytes 159776 | tf_op jit(solution)/shard_map/ppermute | solution.py:42
  80.6 3.9 %collective-permute-start.10 = (bf16[416,256]{1,0:T(8,128)(2,1)S(1)}, bf16[416,256]{1,0:T(8,128)(2,1)S(1)}, u32[]{:S(2)}, u32[]{:S(2)}) collective-permute-start(bf16[416,256]{1,0:T(8,128)(2,1)S(1)} %get-tuple-element.93), channel_id=1, source_target_pairs={{0,32},{32,0},{64,96},{96,64},{128,160},{160,128},{192,224},{224,1... | collective-permute-start | bytes 638984 | tf_op jit(solution)/shard_map/ppermute | solution.py:45
  84.4 3.8 %collective-permute-start.8 = (bf16[24,3328]{1,0:T(8,128)(2,1)S(1)}, bf16[24,3328]{1,0:T(8,128)(2,1)S(1)}, u32[]{:S(2)}, u32[]{:S(2)}) collective-permute-start(bf16[24,3328]{1,0:T(8,128)(2,1)S(1)} %collective-permute-done.5), channel_id=1, source_target_pairs={{0,64},{32,96},{64,128},{96,160},{128,192},{160,224},{192,256},{22... | collective-permute-start | bytes 479240 | tf_op jit(solution)/shard_map/ppermute | solution.py:42
  88.2 3.7 %collective-permute-start.9 = (bf16[24,3328]{1,0:T(8,128)(2,1)S(1)}, bf16[24,3328]{1,0:T(8,128)(2,1)S(1)}, u32[]{:S(2)}, u32[]{:S(2)}) collective-permute-start(bf16[24,3328]{1,0:T(8,128)(2,1)S(1)} %collective-permute-done.6), channel_id=1, source_target_pairs={{0,960},{32,992},{64,0},{96,32},{128,64},{160,96},{192,128},{224,1... | collective-permute-start | bytes 479240 | tf_op jit(solution)/shard_map/ppermute | solution.py:42
  92.0 4.3 %collective-permute-done.8 = bf16[24,3328]{1,0:T(8,128)(2,1)S(1)} collective-permute-done((bf16[24,3328]{1,0:T(8,128)(2,1)S(1)}, bf16[24,3328]{1,0:T(8,128)(2,1)S(1)}, u32[]{:S(2)}, u32[]{:S(2)}) %collective-permute-start.8) | collective-permute-done | bytes 159776 | tf_op jit(solution)/shard_map/ppermute | solution.py:42
  96.3 3.5 %collective-permute-done.9 = bf16[24,3328]{1,0:T(8,128)(2,1)S(1)} collective-permute-done((bf16[24,3328]{1,0:T(8,128)(2,1)S(1)}, bf16[24,3328]{1,0:T(8,128)(2,1)S(1)}, u32[]{:S(2)}, u32[]{:S(2)}) %collective-permute-start.9) | collective-permute-done | bytes 159776 | tf_op jit(solution)/shard_map/ppermute | solution.py:42
  101.8 7.1 %collective-permute-start.11 = (bf16[24,3328]{1,0:T(8,128)(2,1)S(1)}, bf16[24,3328]{1,0:T(8,128)(2,1)S(1)}, u32[]{:S(2)}, u32[]{:S(2)}) collective-permute-start(bf16[24,3328]{1,0:T(8,128)(2,1)S(1)} %collective-permute-done.8), channel_id=1, source_target_pairs={{0,64},{32,96},{64,128},{96,160},{128,192},{160,224},{192,256},{22... | collective-permute-start | bytes 479240 | tf_op jit(solution)/shard_map/ppermute | solution.py:42
  108.9 1.9 collective-permute-start.12
  110.8 3.6 %collective-permute-done.11 = bf16[24,3328]{1,0:T(8,128)(2,1)S(1)} collective-permute-done((bf16[24,3328]{1,0:T(8,128)(2,1)S(1)}, bf16[24,3328]{1,0:T(8,128)(2,1)S(1)}, u32[]{:S(2)}, u32[]{:S(2)}) %collective-permute-start.11) | collective-permute-done | bytes 159776 | tf_op jit(solution)/shard_map/ppermute | solution.py:42
  114.4 3.2 collective-permute-done.12
  117.6 11.8 %collective-permute-start.14 = (bf16[24,3328]{1,0:T(8,128)(2,1)S(1)}, bf16[24,3328]{1,0:T(8,128)(2,1)}, u32[]{:S(2)}, u32[]{:S(2)}) collective-permute-start(bf16[24,3328]{1,0:T(8,128)(2,1)S(1)} %collective-permute-done.11), channel_id=1, source_target_pairs={{0,64},{32,96},{64,128},{96,160},{128,192},{160,224},{192,256},{22... | collective-permute-start | bytes 479240 | tf_op jit(solution)/shard_map/ppermute | solution.py:42
  129.5 1.9 collective-permute-start.15
  131.4 1.9 collective-permute-start.19
  134.0 3.2 collective-permute-done.15
  137.2 6.7 %collective-permute-start.16 = (bf16[24,3328]{1,0:T(8,128)(2,1)}, bf16[24,3328]{1,0:T(8,128)(2,1)S(1)}, u32[]{:S(2)}, u32[]{:S(2)}) collective-permute-start(bf16[24,3328]{1,0:T(8,128)(2,1)} %collective-permute-done.14), channel_id=1, source_target_pairs={{0,64},{32,96},{64,128},{96,160},{128,192},{160,224},{192,256},{22... | collective-permute-start | bytes 479240 | tf_op jit(solution)/shard_map/ppermute | solution.py:42
  146.0 12.3 %collective-permute-done.16 = bf16[24,3328]{1,0:T(8,128)(2,1)S(1)} collective-permute-done((bf16[24,3328]{1,0:T(8,128)(2,1)}, bf16[24,3328]{1,0:T(8,128)(2,1)S(1)}, u32[]{:S(2)}, u32[]{:S(2)}) %collective-permute-start.16) | collective-permute-done | bytes 159776 | tf_op jit(solution)/shard_map/ppermute | solution.py:42
  158.3 4.9 %collective-permute-start.18 = (bf16[24,3328]{1,0:T(8,128)(2,1)S(1)}, bf16[24,3328]{1,0:T(8,128)(2,1)S(1)}, u32[]{:S(2)}, u32[]{:S(2)}) collective-permute-start(bf16[24,3328]{1,0:T(8,128)(2,1)S(1)} %collective-permute-done.16), channel_id=1, source_target_pairs={{0,64},{32,96},{64,128},{96,160},{128,192},{160,224},{192,256},{22... | collective-permute-start | bytes 479240 | tf_op jit(solution)/shard_map/ppermute | solution.py:42
  163.3 3.2 collective-permute-done.18
  170.3 2.1 fusion.22
  178.6 2.2 collective-permute-start.20
  180.8 4.9 %collective-permute-done.20 = f32[24,1664]{1,0:T(8,128)S(1)} collective-permute-done((f32[24,1664]{1,0:T(8,128)S(1)}, f32[24,1664]{1,0:T(8,128)S(1)}, u32[]{:S(2)}, u32[]{:S(2)}) %collective-permute-start.20) | collective-permute-done | bytes 159776 | tf_op jit(solution)/shard_map/ppermute | solution.py:42
  185.8 10.5 %collective-permute-start.23 = (bf16[416,256]{1,0:T(8,128)(2,1)S(1)}, bf16[416,256]{1,0:T(8,128)(2,1)S(1)}, u32[]{:S(2)}, u32[]{:S(2)}) collective-permute-start(bf16[416,256]{1,0:T(8,128)(2,1)S(1)} %get-tuple-element.114), channel_id=1, source_target_pairs={{0,32},{32,0},{64,96},{96,64},{128,160},{160,128},{192,224},{224,1... | collective-permute-start | bytes 638984 | tf_op jit(solution)/shard_map/ppermute | solution.py:45
  196.3 3.0 collective-permute-start.21
  199.3 3.2 collective-permute-start.22
  202.4 2.3 collective-permute-done.21
  204.7 3.4 %collective-permute-done.22 = f32[24,1664]{1,0:T(8,128)S(1)} collective-permute-done((f32[24,1664]{1,0:T(8,128)S(1)}, f32[24,1664]{1,0:T(8,128)S(1)}, u32[]{:S(2)}, u32[]{:S(2)}) %collective-permute-start.22) | collective-permute-done | bytes 159776 | tf_op jit(solution)/shard_map/ppermute | solution.py:42
  208.1 2.7 collective-permute-start.26
  210.8 1.9 collective-permute-start.24
  212.7 4.4 %collective-permute-start.25 = (f32[24,1664]{1,0:T(8,128)S(1)}, f32[24,1664]{1,0:T(8,128)S(1)}, u32[]{:S(2)}, u32[]{:S(2)}) collective-permute-start(f32[24,1664]{1,0:T(8,128)S(1)} %get-tuple-element.118), channel_id=1, source_target_pairs={{0,64},{32,96},{64,128},{96,160},{128,192},{160,224},{192,256},{22... | collective-permute-start | bytes 479240 | tf_op jit(solution)/shard_map/ppermute | solution.py:42
  217.1 2.2 collective-permute-done.24
  219.3 3.2 collective-permute-done.25
  222.6 3.0 collective-permute-start.27
  225.6 3.3 collective-permute-start.28
  229.0 3.6 %collective-permute-start.29 = (bf16[416,256]{1,0:T(8,128)(2,1)S(1)}, bf16[416,256]{1,0:T(8,128)(2,1)S(1)}, u32[]{:S(2)}, u32[]{:S(2)}) collective-permute-start(bf16[416,256]{1,0:T(8,128)(2,1)S(1)} %get-tuple-element.124), channel_id=1, source_target_pairs={{0,32},{32,0},{64,96},{96,64},{128,160},{160,128},{192,224},{224,1... | collective-permute-start | bytes 638984 | tf_op jit(solution)/shard_map/ppermute | solution.py:45
  234.5 4.2 %collective-permute-done.29 = bf16[416,256]{1,0:T(8,128)(2,1)S(1)} collective-permute-done((bf16[416,256]{1,0:T(8,128)(2,1)S(1)}, bf16[416,256]{1,0:T(8,128)(2,1)S(1)}, u32[]{:S(2)}, u32[]{:S(2)}) %collective-permute-start.29) | collective-permute-done | bytes 213024 | tf_op jit(solution)/shard_map/ppermute | solution.py:45
  238.8 3.0 collective-permute-start.30
  241.7 3.8 %collective-permute-start.31 = (f32[24,1664]{1,0:T(8,128)S(1)}, f32[24,1664]{1,0:T(8,128)S(1)}, u32[]{:S(2)}, u32[]{:S(2)}) collective-permute-start(f32[24,1664]{1,0:T(8,128)S(1)} %get-tuple-element.128), channel_id=1, source_target_pairs={{0,64},{32,96},{64,128},{96,160},{128,192},{160,224},{192,256},{22... | collective-permute-start | bytes 479240 | tf_op jit(solution)/shard_map/ppermute | solution.py:42
  245.5 3.7 %collective-permute-start.32 = (bf16[416,256]{1,0:T(8,128)(2,1)S(1)}, bf16[416,256]{1,0:T(8,128)(2,1)S(1)}, u32[]{:S(2)}, u32[]{:S(2)}) collective-permute-start(bf16[416,256]{1,0:T(8,128)(2,1)S(1)} %get-tuple-element.129), channel_id=1, source_target_pairs={{0,32},{32,0},{64,96},{96,64},{128,160},{160,128},{192,224},{224,1... | collective-permute-start | bytes 638984 | tf_op jit(solution)/shard_map/ppermute | solution.py:45
  249.9 4.7 %collective-permute-done.32 = bf16[416,256]{1,0:T(8,128)(2,1)S(1)} collective-permute-done((bf16[416,256]{1,0:T(8,128)(2,1)S(1)}, bf16[416,256]{1,0:T(8,128)(2,1)S(1)}, u32[]{:S(2)}, u32[]{:S(2)}) %collective-permute-start.32) | collective-permute-done | bytes 213024 | tf_op jit(solution)/shard_map/ppermute | solution.py:45
  254.7 3.9 %collective-permute-start.35 = (bf16[80,1664]{1,0:T(8,128)(2,1)S(1)}, bf16[80,1664]{1,0:T(8,128)(2,1)S(1)}, u32[]{:S(2)}, u32[]{:S(2)}) collective-permute-start(bf16[80,1664]{1,0:T(8,128)(2,1)S(1)} %get-tuple-element.134), channel_id=1, source_target_pairs={{0,32},{32,0},{64,96},{96,64},{128,160},{160,128},{192,224},{224,1... | collective-permute-start | bytes 798728 | tf_op jit(solution)/shard_map/ppermute | solution.py:45
  260.5 5.8 %collective-permute-start.34 = (f32[24,1664]{1,0:T(8,128)S(1)}, f32[24,1664]{1,0:T(8,128)S(1)}, u32[]{:S(2)}, u32[]{:S(2)}) collective-permute-start(f32[24,1664]{1,0:T(8,128)S(1)} %get-tuple-element.133), channel_id=1, source_target_pairs={{0,64},{32,96},{64,128},{96,160},{128,192},{160,224},{192,256},{22... | collective-permute-start | bytes 479240 | tf_op jit(solution)/shard_map/ppermute | solution.py:42
  266.3 2.5 collective-permute-done.33
  268.8 2.4 collective-permute-done.34
  273.3 2.3 collective-permute-start.36
  275.5 9.7 %collective-permute-start.37 = (f32[24,1664]{1,0:T(8,128)S(1)}, f32[24,1664]{1,0:T(8,128)S(1)}, u32[]{:S(2)}, u32[]{:S(2)}) collective-permute-start(f32[24,1664]{1,0:T(8,128)S(1)} %get-tuple-element.138), channel_id=1, source_target_pairs={{0,64},{32,96},{64,128},{96,160},{128,192},{160,224},{192,256},{22... | collective-permute-start | bytes 479240 | tf_op jit(solution)/shard_map/ppermute | solution.py:42
  287.6 2.5 collective-permute-start.39
  290.1 6.3 %collective-permute-start.40 = (f32[24,1664]{1,0:T(8,128)S(1)}, f32[24,1664]{1,0:T(8,128)S(1)}, u32[]{:S(2)}, u32[]{:S(2)}) collective-permute-start(f32[24,1664]{1,0:T(8,128)S(1)} %get-tuple-element.143), channel_id=1, source_target_pairs={{0,64},{32,96},{64,128},{96,160},{128,192},{160,224},{192,256},{22... | collective-permute-start | bytes 479240 | tf_op jit(solution)/shard_map/ppermute | solution.py:42
  296.5 2.2 collective-permute-start.41
  300.8 6.5 %collective-permute-done.41 = bf16[96,1664]{1,0:T(8,128)(2,1)} collective-permute-done((bf16[96,1664]{1,0:T(8,128)(2,1)S(1)}, bf16[96,1664]{1,0:T(8,128)(2,1)}, u32[]{:S(2)}, u32[]{:S(2)}) %collective-permute-start.41) | collective-permute-done | bytes 319520 | tf_op jit(solution)/shard_map/ppermute | solution.py:45
  309.0 16.3 %all-to-all-start.1 = ((bf16[32,2,624]{2,1,0:T(2,128)(2,1)}), bf16[32,2,624]{2,1,0:T(2,128)(2,1)S(1)}, u32[]{:S(2)}, u32[]{:S(2)}) async-start(bf16[32,2,624]{2,1,0:T(2,128)(2,1)} %reshape.134), calls=%async_computation.1 | async-start | bytes 163840 | tf_op jit(solution)/shard_map/all_to_all | solution.py:140
  325.3 2.7 fusion.2
  328.1 4.6 %all-to-all-done.1 = bf16[32,2,624]{2,1,0:T(2,128)(2,1)S(1)} async-done(((bf16[32,2,624]{2,1,0:T(2,128)(2,1)}), bf16[32,2,624]{2,1,0:T(2,128)(2,1)S(1)}, u32[]{:S(2)}, u32[]{:S(2)}) %all-to-all-start.1) | async-done | bytes 79904 | tf_op jit(solution)/shard_map/all_to_all | solution.py:140
  (170 shorter events, 38.1 us)
Async XLA Ops:
  0.6 41.5 %copy-start = (bf16[1,1664,256]{2,1,0:T(8,128)(2,1)S(1)}, bf16[1,1664,256]{2,1,0:T(8,128)(2,1)}, u32[]{:S(2)}) copy-start(bf16[1,1664,256]{2,1,0:T(8,128)(2,1)} %param.14) | copy-start | bytes 2555908
  3.5 26.1 %all-to-all-start = ((bf16[32,24,104]{2,1,0:T(8,128)(2,1)}), bf16[32,24,104]{2,1,0:T(8,128)(2,1)S(1)}, u32[]{:S(2)}, u32[]{:S(2)}) async-start(bf16[32,24,104]{2,1,0:T(8,128)(2,1)} %bitcast), calls=%async_computation | async-start | bytes 393216 | tf_op jit(solution)/shard_map/all_to_all | solution.py:59
  30.6 14.6 %collective-permute-start = (bf16[24,3328]{1,0:T(8,128)(2,1)S(1)}, bf16[24,3328]{1,0:T(8,128)(2,1)S(1)}, u32[]{:S(2)}, u32[]{:S(2)}) collective-permute-start(bf16[24,3328]{1,0:T(8,128)(2,1)S(1)} %broadcast_select_fusion.1), channel_id=1, source_target_pairs={{0,64},{32,96},{64,128},{96,160},{128,192},{160,224},{192,256},{22... | collective-permute-start | bytes 479240 | tf_op jit(solution)/shard_map/ppermute | solution.py:42
  32.5 16.5 %collective-permute-start.1 = (bf16[24,3328]{1,0:T(8,128)(2,1)S(1)}, bf16[24,3328]{1,0:T(8,128)(2,1)S(1)}, u32[]{:S(2)}, u32[]{:S(2)}) collective-permute-start(bf16[24,3328]{1,0:T(8,128)(2,1)S(1)} %broadcast_select_fusion.1), channel_id=1, source_target_pairs={{0,960},{32,992},{64,0},{96,32},{128,64},{160,96},{192,128},{224,1... | collective-permute-start | bytes 479240 | tf_op jit(solution)/shard_map/ppermute | solution.py:42
  45.2 86.2 %copy-start.8 = (bf16[24,3328]{1,0:T(8,128)(2,1)}, bf16[24,3328]{1,0:T(8,128)(2,1)S(1)}, u32[]{:S(2)}) copy-start(bf16[24,3328]{1,0:T(8,128)(2,1)S(1)} %collective-permute-done) | copy-start | bytes 479236
  49.0 17.8 %collective-permute-start.4 = (bf16[416,256]{1,0:T(8,128)(2,1)S(1)}, bf16[416,256]{1,0:T(8,128)(2,1)S(1)}, u32[]{:S(2)}, u32[]{:S(2)}) collective-permute-start(bf16[416,256]{1,0:T(8,128)(2,1)S(1)} %get-tuple-element.83), channel_id=1, source_target_pairs={{0,32},{32,0},{64,96},{96,64},{128,160},{160,128},{192,224},{224,1... | collective-permute-start | bytes 638984 | tf_op jit(solution)/shard_map/ppermute | solution.py:45
  50.9 15.9 %collective-permute-start.2 = (bf16[24,3328]{1,0:T(8,128)(2,1)S(1)}, bf16[24,3328]{1,0:T(8,128)(2,1)S(1)}, u32[]{:S(2)}, u32[]{:S(2)}) collective-permute-start(bf16[24,3328]{1,0:T(8,128)(2,1)S(1)} %collective-permute-done), channel_id=1, source_target_pairs={{0,64},{32,96},{64,128},{96,160},{128,192},{160,224},{192,256},{22... | collective-permute-start | bytes 479240 | tf_op jit(solution)/shard_map/ppermute | solution.py:42
  52.8 13.9 %collective-permute-start.3 = (bf16[24,3328]{1,0:T(8,128)(2,1)S(1)}, bf16[24,3328]{1,0:T(8,128)(2,1)S(1)}, u32[]{:S(2)}, u32[]{:S(2)}) collective-permute-start(bf16[24,3328]{1,0:T(8,128)(2,1)S(1)} %collective-permute-done.1), channel_id=1, source_target_pairs={{0,960},{32,992},{64,0},{96,32},{128,64},{160,96},{192,128},{224,1... | collective-permute-start | bytes 479240 | tf_op jit(solution)/shard_map/ppermute | solution.py:42
  66.8 13.7 %collective-permute-start.7 = (bf16[416,256]{1,0:T(8,128)(2,1)S(1)}, bf16[416,256]{1,0:T(8,128)(2,1)S(1)}, u32[]{:S(2)}, u32[]{:S(2)}) collective-permute-start(bf16[416,256]{1,0:T(8,128)(2,1)S(1)} %get-tuple-element.88), channel_id=1, source_target_pairs={{0,32},{32,0},{64,96},{96,64},{128,160},{160,128},{192,224},{224,1... | collective-permute-start | bytes 638984 | tf_op jit(solution)/shard_map/ppermute | solution.py:45
  68.7 11.8 %collective-permute-start.5 = (bf16[24,3328]{1,0:T(8,128)(2,1)S(1)}, bf16[24,3328]{1,0:T(8,128)(2,1)S(1)}, u32[]{:S(2)}, u32[]{:S(2)}) collective-permute-start(bf16[24,3328]{1,0:T(8,128)(2,1)S(1)} %collective-permute-done.2), channel_id=1, source_target_pairs={{0,64},{32,96},{64,128},{96,160},{128,192},{160,224},{192,256},{22... | collective-permute-start | bytes 479240 | tf_op jit(solution)/shard_map/ppermute | solution.py:42
  70.6 9.9 %collective-permute-start.6 = (bf16[24,3328]{1,0:T(8,128)(2,1)S(1)}, bf16[24,3328]{1,0:T(8,128)(2,1)S(1)}, u32[]{:S(2)}, u32[]{:S(2)}) collective-permute-start(bf16[24,3328]{1,0:T(8,128)(2,1)S(1)} %collective-permute-done.3), channel_id=1, source_target_pairs={{0,960},{32,992},{64,0},{96,32},{128,64},{160,96},{192,128},{224,1... | collective-permute-start | bytes 479240 | tf_op jit(solution)/shard_map/ppermute | solution.py:42
  80.5 50.9 %copy-start.16 = (bf16[24,3328]{1,0:T(8,128)(2,1)}, bf16[24,3328]{1,0:T(8,128)(2,1)S(1)}, u32[]{:S(2)}) copy-start(bf16[24,3328]{1,0:T(8,128)(2,1)S(1)} %collective-permute-done.5) | copy-start | bytes 479236
  80.5 50.9 %copy-start.14 = (bf16[24,3328]{1,0:T(8,128)(2,1)}, bf16[24,3328]{1,0:T(8,128)(2,1)S(1)}, u32[]{:S(2)}) copy-start(bf16[24,3328]{1,0:T(8,128)(2,1)S(1)} %collective-permute-done.6) | copy-start | bytes 479236
  80.6 19.3 %collective-permute-start.10 = (bf16[416,256]{1,0:T(8,128)(2,1)S(1)}, bf16[416,256]{1,0:T(8,128)(2,1)S(1)}, u32[]{:S(2)}, u32[]{:S(2)}) collective-permute-start(bf16[416,256]{1,0:T(8,128)(2,1)S(1)} %get-tuple-element.93), channel_id=1, source_target_pairs={{0,32},{32,0},{64,96},{96,64},{128,160},{160,128},{192,224},{224,1... | collective-permute-start | bytes 638984 | tf_op jit(solution)/shard_map/ppermute | solution.py:45
  84.4 11.9 %collective-permute-start.8 = (bf16[24,3328]{1,0:T(8,128)(2,1)S(1)}, bf16[24,3328]{1,0:T(8,128)(2,1)S(1)}, u32[]{:S(2)}, u32[]{:S(2)}) collective-permute-start(bf16[24,3328]{1,0:T(8,128)(2,1)S(1)} %collective-permute-done.5), channel_id=1, source_target_pairs={{0,64},{32,96},{64,128},{96,160},{128,192},{160,224},{192,256},{22... | collective-permute-start | bytes 479240 | tf_op jit(solution)/shard_map/ppermute | solution.py:42
  88.2 11.6 %collective-permute-start.9 = (bf16[24,3328]{1,0:T(8,128)(2,1)S(1)}, bf16[24,3328]{1,0:T(8,128)(2,1)S(1)}, u32[]{:S(2)}, u32[]{:S(2)}) collective-permute-start(bf16[24,3328]{1,0:T(8,128)(2,1)S(1)} %collective-permute-done.6), channel_id=1, source_target_pairs={{0,960},{32,992},{64,0},{96,32},{128,64},{160,96},{192,128},{224,1... | collective-permute-start | bytes 479240 | tf_op jit(solution)/shard_map/ppermute | solution.py:42
  96.3 35.1 %copy-start.22 = (bf16[24,3328]{1,0:T(8,128)(2,1)}, bf16[24,3328]{1,0:T(8,128)(2,1)S(1)}, u32[]{:S(2)}) copy-start(bf16[24,3328]{1,0:T(8,128)(2,1)S(1)} %collective-permute-done.8) | copy-start | bytes 479236
  99.9 31.6 %copy-start.18 = (bf16[24,3328]{1,0:T(8,128)(2,1)}, bf16[24,3328]{1,0:T(8,128)(2,1)S(1)}, u32[]{:S(2)}) copy-start(bf16[24,3328]{1,0:T(8,128)(2,1)S(1)} %collective-permute-done.9) | copy-start | bytes 479236
  99.9 17.8 %collective-permute-start.13 = (bf16[416,256]{1,0:T(8,128)(2,1)S(1)}, bf16[416,256]{1,0:T(8,128)(2,1)S(1)}, u32[]{:S(2)}, u32[]{:S(2)}) collective-permute-start(bf16[416,256]{1,0:T(8,128)(2,1)S(1)} %get-tuple-element.98), channel_id=1, source_target_pairs={{0,32},{32,0},{64,96},{96,64},{128,160},{160,128},{192,224},{224,1... | collective-permute-start | bytes 638984 | tf_op jit(solution)/shard_map/ppermute | solution.py:45
  101.8 12.7 %collective-permute-start.11 = (bf16[24,3328]{1,0:T(8,128)(2,1)S(1)}, bf16[24,3328]{1,0:T(8,128)(2,1)S(1)}, u32[]{:S(2)}, u32[]{:S(2)}) collective-permute-start(bf16[24,3328]{1,0:T(8,128)(2,1)S(1)} %collective-permute-done.8), channel_id=1, source_target_pairs={{0,64},{32,96},{64,128},{96,160},{128,192},{160,224},{192,256},{22... | collective-permute-start | bytes 479240 | tf_op jit(solution)/shard_map/ppermute | solution.py:42
  108.9 8.7 %collective-permute-start.12 = (bf16[24,3328]{1,0:T(8,128)(2,1)S(1)}, bf16[24,3328]{1,0:T(8,128)(2,1)S(1)}, u32[]{:S(2)}, u32[]{:S(2)}) collective-permute-start(bf16[24,3328]{1,0:T(8,128)(2,1)S(1)} %collective-permute-done.9), channel_id=1, source_target_pairs={{0,960},{32,992},{64,0},{96,32},{128,64},{160,96},{192,128},{224,1... | collective-permute-start | bytes 479240 | tf_op jit(solution)/shard_map/ppermute | solution.py:42
  114.4 29.5 %copy-start.24 = (bf16[24,3328]{1,0:T(8,128)(2,1)}, bf16[24,3328]{1,0:T(8,128)(2,1)S(1)}, u32[]{:S(2)}) copy-start(bf16[24,3328]{1,0:T(8,128)(2,1)S(1)} %collective-permute-done.11) | copy-start | bytes 479236
  117.6 26.3 %copy-start.20 = (bf16[24,3328]{1,0:T(8,128)(2,1)}, bf16[24,3328]{1,0:T(8,128)(2,1)S(1)}, u32[]{:S(2)}) copy-start(bf16[24,3328]{1,0:T(8,128)(2,1)S(1)} %collective-permute-done.12) | copy-start | bytes 479236
  117.6 16.4 %collective-permute-start.14 = (bf16[24,3328]{1,0:T(8,128)(2,1)S(1)}, bf16[24,3328]{1,0:T(8,128)(2,1)}, u32[]{:S(2)}, u32[]{:S(2)}) collective-permute-start(bf16[24,3328]{1,0:T(8,128)(2,1)S(1)} %collective-permute-done.11), channel_id=1, source_target_pairs={{0,64},{32,96},{64,128},{96,160},{128,192},{160,224},{192,256},{22... | collective-permute-start | bytes 479240 | tf_op jit(solution)/shard_map/ppermute | solution.py:42
  129.5 7.8 %collective-permute-start.15 = (bf16[24,3328]{1,0:T(8,128)(2,1)S(1)}, bf16[24,3328]{1,0:T(8,128)(2,1)}, u32[]{:S(2)}, u32[]{:S(2)}) collective-permute-start(bf16[24,3328]{1,0:T(8,128)(2,1)S(1)} %collective-permute-done.12), channel_id=1, source_target_pairs={{0,960},{32,992},{64,0},{96,32},{128,64},{160,96},{192,128},{224,1... | collective-permute-start | bytes 479240 | tf_op jit(solution)/shard_map/ppermute | solution.py:42
  131.4 42.4 %collective-permute-start.19 = (bf16[256,1664]{1,0:T(8,128)(2,1)}, bf16[256,1664]{1,0:T(8,128)(2,1)}, u32[]{:S(2)}, u32[]{:S(2)}) collective-permute-start(bf16[256,1664]{1,0:T(8,128)(2,1)} %bitcast.153), channel_id=1, source_target_pairs={{0,32},{32,0},{64,96},{96,64},{128,160},{160,128},{192,224},{224,1... | collective-permute-start | bytes 2555912 | tf_op jit(solution)/shard_map/ppermute | solution.py:45
  134.0 33.5 %copy-start.23 = (bf16[24,3328]{1,0:T(8,128)(2,1)S(1)}, bf16[24,3328]{1,0:T(8,128)(2,1)}, u32[]{:S(2)}) copy-start(bf16[24,3328]{1,0:T(8,128)(2,1)} %copy-done.22) | copy-start | bytes 479236
  134.0 33.5 %copy-start.17 = (bf16[24,3328]{1,0:T(8,128)(2,1)S(1)}, bf16[24,3328]{1,0:T(8,128)(2,1)}, u32[]{:S(2)}) copy-start(bf16[24,3328]{1,0:T(8,128)(2,1)} %copy-done.16) | copy-start | bytes 479236
  134.0 33.5 %copy-start.13 = (bf16[24,3328]{1,0:T(8,128)(2,1)S(1)}, bf16[24,3328]{1,0:T(8,128)(2,1)}, u32[]{:S(2)}) copy-start(bf16[24,3328]{1,0:T(8,128)(2,1)} %copy-done.12) | copy-start | bytes 479236
  134.0 33.6 %copy-start.9 = (bf16[24,3328]{1,0:T(8,128)(2,1)S(1)}, bf16[24,3328]{1,0:T(8,128)(2,1)}, u32[]{:S(2)}) copy-start(bf16[24,3328]{1,0:T(8,128)(2,1)} %copy-done.8) | copy-start | bytes 479236
  134.0 33.7 %copy-start.11 = (bf16[24,3328]{1,0:T(8,128)(2,1)S(1)}, bf16[24,3328]{1,0:T(8,128)(2,1)}, u32[]{:S(2)}) copy-start(bf16[24,3328]{1,0:T(8,128)(2,1)} %copy-done.10) | copy-start | bytes 479236
  134.0 33.7 %copy-start.15 = (bf16[24,3328]{1,0:T(8,128)(2,1)S(1)}, bf16[24,3328]{1,0:T(8,128)(2,1)}, u32[]{:S(2)}) copy-start(bf16[24,3328]{1,0:T(8,128)(2,1)} %copy-done.14) | copy-start | bytes 479236
  137.2 21.1 %collective-permute-start.16 = (bf16[24,3328]{1,0:T(8,128)(2,1)}, bf16[24,3328]{1,0:T(8,128)(2,1)S(1)}, u32[]{:S(2)}, u32[]{:S(2)}) collective-permute-start(bf16[24,3328]{1,0:T(8,128)(2,1)} %collective-permute-done.14), channel_id=1, source_target_pairs={{0,64},{32,96},{64,128},{96,160},{128,192},{160,224},{192,256},{22... | collective-permute-start | bytes 479240 | tf_op jit(solution)/shard_map/ppermute | solution.py:42
  144.0 14.4 %collective-permute-start.17 = (bf16[24,3328]{1,0:T(8,128)(2,1)}, bf16[24,3328]{1,0:T(8,128)(2,1)S(1)}, u32[]{:S(2)}, u32[]{:S(2)}) collective-permute-start(bf16[24,3328]{1,0:T(8,128)(2,1)} %collective-permute-done.15), channel_id=1, source_target_pairs={{0,960},{32,992},{64,0},{96,32},{128,64},{160,96},{192,128},{224,1... | collective-permute-start | bytes 479240 | tf_op jit(solution)/shard_map/ppermute | solution.py:42
  145.9 21.8 %copy-start.19 = (bf16[24,3328]{1,0:T(8,128)(2,1)S(1)}, bf16[24,3328]{1,0:T(8,128)(2,1)}, u32[]{:S(2)}) copy-start(bf16[24,3328]{1,0:T(8,128)(2,1)} %copy-done.18) | copy-start | bytes 479236
  158.3 8.1 %collective-permute-start.18 = (bf16[24,3328]{1,0:T(8,128)(2,1)S(1)}, bf16[24,3328]{1,0:T(8,128)(2,1)S(1)}, u32[]{:S(2)}, u32[]{:S(2)}) collective-permute-start(bf16[24,3328]{1,0:T(8,128)(2,1)S(1)} %collective-permute-done.16), channel_id=1, source_target_pairs={{0,64},{32,96},{64,128},{96,160},{128,192},{160,224},{192,256},{22... | collective-permute-start | bytes 479240 | tf_op jit(solution)/shard_map/ppermute | solution.py:42
  178.5 54.0 %copy-start.3 = (f32[384,256]{0,1:T(8,128)S(1)}, f32[384,256]{0,1:T(8,128)}, u32[]{:S(2)}) copy-start(f32[384,256]{0,1:T(8,128)} %copy-done.2) | copy-start | bytes 1179652
  178.5 54.0 %copy-start.28 = (bf16[16,24,3328]{2,1,0:T(8,128)(2,1)S(1)}, bf16[16,24,3328]{2,1,0:T(8,128)(2,1)}, u32[]{:S(2)}) copy-start(bf16[16,24,3328]{2,1,0:T(8,128)(2,1)} %copy-done.26) | copy-start | bytes 7667716
  178.6 7.2 %collective-permute-start.20 = (f32[24,1664]{1,0:T(8,128)S(1)}, f32[24,1664]{1,0:T(8,128)S(1)}, u32[]{:S(2)}, u32[]{:S(2)}) collective-permute-start(f32[24,1664]{1,0:T(8,128)S(1)} %get-tuple-element.110), channel_id=1, source_target_pairs={{0,960},{32,992},{64,0},{96,32},{128,64},{160,96},{192,128},{224,1... | collective-permute-start | bytes 479240 | tf_op jit(solution)/shard_map/ppermute | solution.py:42
  185.8 22.3 %collective-permute-start.23 = (bf16[416,256]{1,0:T(8,128)(2,1)S(1)}, bf16[416,256]{1,0:T(8,128)(2,1)S(1)}, u32[]{:S(2)}, u32[]{:S(2)}) collective-permute-start(bf16[416,256]{1,0:T(8,128)(2,1)S(1)} %get-tuple-element.114), channel_id=1, source_target_pairs={{0,32},{32,0},{64,96},{96,64},{128,160},{160,128},{192,224},{224,1... | collective-permute-start | bytes 638984 | tf_op jit(solution)/shard_map/ppermute | solution.py:45
  196.3 8.5 %collective-permute-start.21 = (f32[24,1664]{1,0:T(8,128)S(1)}, f32[24,1664]{1,0:T(8,128)S(1)}, u32[]{:S(2)}, u32[]{:S(2)}) collective-permute-start(f32[24,1664]{1,0:T(8,128)S(1)} %fusion.59), channel_id=1, source_target_pairs={{0,960},{32,992},{64,0},{96,32},{128,64},{160,96},{192,128},{224,1... | collective-permute-start | bytes 479240 | tf_op jit(solution)/shard_map/ppermute | solution.py:42
  199.3 8.8 %collective-permute-start.22 = (f32[24,1664]{1,0:T(8,128)S(1)}, f32[24,1664]{1,0:T(8,128)S(1)}, u32[]{:S(2)}, u32[]{:S(2)}) collective-permute-start(f32[24,1664]{1,0:T(8,128)S(1)} %get-tuple-element.113), channel_id=1, source_target_pairs={{0,64},{32,96},{64,128},{96,160},{128,192},{160,224},{192,256},{22... | collective-permute-start | bytes 479240 | tf_op jit(solution)/shard_map/ppermute | solution.py:42
  208.1 14.4 %collective-permute-start.26 = (bf16[416,256]{1,0:T(8,128)(2,1)S(1)}, bf16[416,256]{1,0:T(8,128)(2,1)S(1)}, u32[]{:S(2)}, u32[]{:S(2)}) collective-permute-start(bf16[416,256]{1,0:T(8,128)(2,1)S(1)} %get-tuple-element.119), channel_id=1, source_target_pairs={{0,32},{32,0},{64,96},{96,64},{128,160},{160,128},{192,224},{224,1... | collective-permute-start | bytes 638984 | tf_op jit(solution)/shard_map/ppermute | solution.py:45
  210.8 8.5 %collective-permute-start.24 = (f32[24,1664]{1,0:T(8,128)S(1)}, f32[24,1664]{1,0:T(8,128)S(1)}, u32[]{:S(2)}, u32[]{:S(2)}) collective-permute-start(f32[24,1664]{1,0:T(8,128)S(1)} %get-tuple-element.117), channel_id=1, source_target_pairs={{0,960},{32,992},{64,0},{96,32},{128,64},{160,96},{192,128},{224,1... | collective-permute-start | bytes 479240 | tf_op jit(solution)/shard_map/ppermute | solution.py:42
  212.7 9.8 %collective-permute-start.25 = (f32[24,1664]{1,0:T(8,128)S(1)}, f32[24,1664]{1,0:T(8,128)S(1)}, u32[]{:S(2)}, u32[]{:S(2)}) collective-permute-start(f32[24,1664]{1,0:T(8,128)S(1)} %get-tuple-element.118), channel_id=1, source_target_pairs={{0,64},{32,96},{64,128},{96,160},{128,192},{160,224},{192,256},{22... | collective-permute-start | bytes 479240 | tf_op jit(solution)/shard_map/ppermute | solution.py:42
  222.6 10.7 %collective-permute-start.27 = (f32[24,1664]{1,0:T(8,128)S(1)}, f32[24,1664]{1,0:T(8,128)S(1)}, u32[]{:S(2)}, u32[]{:S(2)}) collective-permute-start(f32[24,1664]{1,0:T(8,128)S(1)} %get-tuple-element.122), channel_id=1, source_target_pairs={{0,960},{32,992},{64,0},{96,32},{128,64},{160,96},{192,128},{224,1... | collective-permute-start | bytes 479240 | tf_op jit(solution)/shard_map/ppermute | solution.py:42
  225.6 8.8 %collective-permute-start.28 = (f32[24,1664]{1,0:T(8,128)S(1)}, f32[24,1664]{1,0:T(8,128)S(1)}, u32[]{:S(2)}, u32[]{:S(2)}) collective-permute-start(f32[24,1664]{1,0:T(8,128)S(1)} %get-tuple-element.123), channel_id=1, source_target_pairs={{0,64},{32,96},{64,128},{96,160},{128,192},{160,224},{192,256},{22... | collective-permute-start | bytes 479240 | tf_op jit(solution)/shard_map/ppermute | solution.py:42
  229.0 9.8 %collective-permute-start.29 = (bf16[416,256]{1,0:T(8,128)(2,1)S(1)}, bf16[416,256]{1,0:T(8,128)(2,1)S(1)}, u32[]{:S(2)}, u32[]{:S(2)}) collective-permute-start(bf16[416,256]{1,0:T(8,128)(2,1)S(1)} %get-tuple-element.124), channel_id=1, source_target_pairs={{0,32},{32,0},{64,96},{96,64},{128,160},{160,128},{192,224},{224,1... | collective-permute-start | bytes 638984 | tf_op jit(solution)/shard_map/ppermute | solution.py:45
  233.3 65.4 %copy-start.5 = (f32[384,256]{0,1:T(8,128)S(1)}, f32[384,256]{0,1:T(8,128)}, u32[]{:S(2)}) copy-start(f32[384,256]{0,1:T(8,128)} %copy-done.4) | copy-start | bytes 1179652
  233.3 65.3 %copy-start.7 = (f32[384,256]{0,1:T(8,128)S(1)}, f32[384,256]{0,1:T(8,128)}, u32[]{:S(2)}) copy-start(f32[384,256]{0,1:T(8,128)} %copy-done.6) | copy-start | bytes 1179652
  238.8 10.5 %collective-permute-start.30 = (f32[24,1664]{1,0:T(8,128)S(1)}, f32[24,1664]{1,0:T(8,128)S(1)}, u32[]{:S(2)}, u32[]{:S(2)}) collective-permute-start(f32[24,1664]{1,0:T(8,128)S(1)} %get-tuple-element.127), channel_id=1, source_target_pairs={{0,960},{32,992},{64,0},{96,32},{128,64},{160,96},{192,128},{224,1... | collective-permute-start | bytes 479240 | tf_op jit(solution)/shard_map/ppermute | solution.py:42
  241.7 8.2 %collective-permute-start.31 = (f32[24,1664]{1,0:T(8,128)S(1)}, f32[24,1664]{1,0:T(8,128)S(1)}, u32[]{:S(2)}, u32[]{:S(2)}) collective-permute-start(f32[24,1664]{1,0:T(8,128)S(1)} %get-tuple-element.128), channel_id=1, source_target_pairs={{0,64},{32,96},{64,128},{96,160},{128,192},{160,224},{192,256},{22... | collective-permute-start | bytes 479240 | tf_op jit(solution)/shard_map/ppermute | solution.py:42
  245.5 9.2 %collective-permute-start.32 = (bf16[416,256]{1,0:T(8,128)(2,1)S(1)}, bf16[416,256]{1,0:T(8,128)(2,1)S(1)}, u32[]{:S(2)}, u32[]{:S(2)}) collective-permute-start(bf16[416,256]{1,0:T(8,128)(2,1)S(1)} %get-tuple-element.129), channel_id=1, source_target_pairs={{0,32},{32,0},{64,96},{96,64},{128,160},{160,128},{192,224},{224,1... | collective-permute-start | bytes 638984 | tf_op jit(solution)/shard_map/ppermute | solution.py:45
  254.7 16.5 %collective-permute-start.35 = (bf16[80,1664]{1,0:T(8,128)(2,1)S(1)}, bf16[80,1664]{1,0:T(8,128)(2,1)S(1)}, u32[]{:S(2)}, u32[]{:S(2)}) collective-permute-start(bf16[80,1664]{1,0:T(8,128)(2,1)S(1)} %get-tuple-element.134), channel_id=1, source_target_pairs={{0,32},{32,0},{64,96},{96,64},{128,160},{160,128},{192,224},{224,1... | collective-permute-start | bytes 798728 | tf_op jit(solution)/shard_map/ppermute | solution.py:45
  258.6 10.2 %collective-permute-start.33 = (f32[24,1664]{1,0:T(8,128)S(1)}, f32[24,1664]{1,0:T(8,128)S(1)}, u32[]{:S(2)}, u32[]{:S(2)}) collective-permute-start(f32[24,1664]{1,0:T(8,128)S(1)} %get-tuple-element.132), channel_id=1, source_target_pairs={{0,960},{32,992},{64,0},{96,32},{128,64},{160,96},{192,128},{224,1... | collective-permute-start | bytes 479240 | tf_op jit(solution)/shard_map/ppermute | solution.py:42
  260.5 10.7 %collective-permute-start.34 = (f32[24,1664]{1,0:T(8,128)S(1)}, f32[24,1664]{1,0:T(8,128)S(1)}, u32[]{:S(2)}, u32[]{:S(2)}) collective-permute-start(f32[24,1664]{1,0:T(8,128)S(1)} %get-tuple-element.133), channel_id=1, source_target_pairs={{0,64},{32,96},{64,128},{96,160},{128,192},{160,224},{192,256},{22... | collective-permute-start | bytes 479240 | tf_op jit(solution)/shard_map/ppermute | solution.py:42
  271.3 25.2 %copy-start.30 = (bf16[80,1664]{1,0:T(8,128)(2,1)}, bf16[80,1664]{1,0:T(8,128)(2,1)S(1)}, u32[]{:S(2)}) copy-start(bf16[80,1664]{1,0:T(8,128)(2,1)S(1)} %collective-permute-done.35) | copy-start | bytes 798724
  271.3 16.2 %collective-permute-start.38 = (bf16[80,1664]{1,0:T(8,128)(2,1)S(1)}, bf16[80,1664]{1,0:T(8,128)(2,1)S(1)}, u32[]{:S(2)}, u32[]{:S(2)}) collective-permute-start(bf16[80,1664]{1,0:T(8,128)(2,1)S(1)} %get-tuple-element.139), channel_id=1, source_target_pairs={{0,32},{32,0},{64,96},{96,64},{128,160},{160,128},{192,224},{224,1... | collective-permute-start | bytes 798728 | tf_op jit(solution)/shard_map/ppermute | solution.py:45
  273.3 13.7 %collective-permute-start.36 = (f32[24,1664]{1,0:T(8,128)S(1)}, f32[24,1664]{1,0:T(8,128)S(1)}, u32[]{:S(2)}, u32[]{:S(2)}) collective-permute-start(f32[24,1664]{1,0:T(8,128)S(1)} %get-tuple-element.137), channel_id=1, source_target_pairs={{0,960},{32,992},{64,0},{96,32},{128,64},{160,96},{192,128},{224,1... | collective-permute-start | bytes 479240 | tf_op jit(solution)/shard_map/ppermute | solution.py:42
  275.5 12.0 %collective-permute-start.37 = (f32[24,1664]{1,0:T(8,128)S(1)}, f32[24,1664]{1,0:T(8,128)S(1)}, u32[]{:S(2)}, u32[]{:S(2)}) collective-permute-start(f32[24,1664]{1,0:T(8,128)S(1)} %get-tuple-element.138), channel_id=1, source_target_pairs={{0,64},{32,96},{64,128},{96,160},{128,192},{160,224},{192,256},{22... | collective-permute-start | bytes 479240 | tf_op jit(solution)/shard_map/ppermute | solution.py:42
  287.6 12.7 %collective-permute-start.39 = (f32[24,1664]{1,0:T(8,128)S(1)}, f32[24,1664]{1,0:T(8,128)S(1)}, u32[]{:S(2)}, u32[]{:S(2)}) collective-permute-start(f32[24,1664]{1,0:T(8,128)S(1)} %get-tuple-element.142), channel_id=1, source_target_pairs={{0,960},{32,992},{64,0},{96,32},{128,64},{160,96},{192,128},{224,1... | collective-permute-start | bytes 479240 | tf_op jit(solution)/shard_map/ppermute | solution.py:42
  290.1 10.7 %collective-permute-start.40 = (f32[24,1664]{1,0:T(8,128)S(1)}, f32[24,1664]{1,0:T(8,128)S(1)}, u32[]{:S(2)}, u32[]{:S(2)}) collective-permute-start(f32[24,1664]{1,0:T(8,128)S(1)} %get-tuple-element.143), channel_id=1, source_target_pairs={{0,64},{32,96},{64,128},{96,160},{128,192},{160,224},{192,256},{22... | collective-permute-start | bytes 479240 | tf_op jit(solution)/shard_map/ppermute | solution.py:42
  296.5 10.8 %collective-permute-start.41 = (bf16[96,1664]{1,0:T(8,128)(2,1)S(1)}, bf16[96,1664]{1,0:T(8,128)(2,1)}, u32[]{:S(2)}, u32[]{:S(2)}) collective-permute-start(bf16[96,1664]{1,0:T(8,128)(2,1)S(1)} %slice.186), channel_id=1, source_target_pairs={{0,32},{32,0},{64,96},{96,64},{128,160},{160,128},{192,224},{224,1... | collective-permute-start | bytes 958472 | tf_op jit(solution)/shard_map/ppermute | solution.py:45
  309.0 23.6 %all-to-all-start.1 = ((bf16[32,2,624]{2,1,0:T(2,128)(2,1)}), bf16[32,2,624]{2,1,0:T(2,128)(2,1)S(1)}, u32[]{:S(2)}, u32[]{:S(2)}) async-start(bf16[32,2,624]{2,1,0:T(2,128)(2,1)} %reshape.134), calls=%async_computation.1 | async-start | bytes 163840 | tf_op jit(solution)/shard_map/all_to_all | solution.py:140
  (12 other events, 100.8 us)

commit v3 on v2

--- a/solution.py
+++ b/solution.py
@@ -19,18 +19,11 @@
     return lax.dot_general(left, right, ((dims[0], dims[1]), ((), ())), preferred_element_type=F32)
 
 
-def pieces(values, cuts):
-    sizes = [values.shape[0] // cuts // 16 * 16] * (cuts - 1)
-    sizes.append(values.shape[0] - sum(sizes))
-    starts = [sum(sizes[:i]) for i in range(cuts)]
-    return [values[at:at + size] for at, size in zip(starts, sizes)]
-
-
 def body(tokens, cotangent, gate_values, route_ids, route_slots, kept_mask, weight_in, weight_out):
     experts = lax.axis_size("expert")
     dp = lax.axis_size("dp")
     ring = dp // 2
-    half = ring // 2
+    groups = [list(range(0, dp, 2)), list(range(1, dp, 2))]
     tok_rows, piece = tokens.shape
     width = piece * experts
     top = route_ids.shape[1]
@@ -38,14 +31,11 @@
     pad = (cap + 1 + 7) // 8 * 8
     me = lax.axis_index("expert")
 
-    def shift(values, by):
-        return lax.ppermute(values, "dp", [(i, (i + by) % dp) for i in range(dp)])
-
     def swap(values):
         return lax.ppermute(values, "dp", [(i, i ^ 1) for i in range(dp)])
 
     own_in, own_out = weight_in[0], weight_out[0]
-    mate_out = swap(own_out)
+    mate_in, mate_out = swap(own_in), swap(own_out)
 
     kept = kept_mask == 1
     target = jnp.where(kept, route_ids * pad + route_slots, -1)
@@ -65,26 +55,7 @@
     spare = lax.broadcasted_iota(jnp.int32, (pad, 2 * width), 0) == cap
     block = jnp.where(spare, own_gates.astype(BF16)[None, :], arrived)
 
-    found = {0: block}
-    ahead = behind = block
-    queue, mate_in = pieces(own_in, 4), []
-    for step in range(half):
-        sent = [queue.pop(0)] if queue and step > 0 else []
-        ahead, behind, *sent = lax.optimization_barrier((ahead, behind, *sent))
-        ahead = shift(ahead, 2)
-        found[-step - 1] = ahead
-        if step + 1 < ring - half:
-            behind = shift(behind, -2)
-            found[step + 1] = behind
-        if sent:
-            got = swap(sent[0])
-            ahead, behind, got = lax.optimization_barrier((ahead, behind, got))
-            mate_in.append(got)
-    while queue:
-        mate_in.append(swap(queue.pop(0)))
-    mate_in = jnp.concatenate(mate_in, axis=0)
-    order = sorted(found)
-    gathered = jnp.stack([found[at] for at in order])
+    gathered = lax.all_gather(block, "dp", axis=0, axis_index_groups=groups)
     gates = jnp.pad(gathered[:, cap, :cap].astype(F32), ((0, 0), (0, pad - cap))).reshape(ring * pad, 1)
     gathered = gathered.reshape(ring * pad, 2 * width)
     rows, grads = gathered[:, :width], gathered[:, width:]
@@ -103,33 +74,11 @@
     gate_terms = jnp.pad(gate_terms.reshape(ring, pad)[:, :cap], ((0, 0), (0, width - cap)))
     spare_row = lax.broadcasted_iota(jnp.int32, (1, pad, 1), 1) == cap
     terms = jnp.where(spare_row, gate_terms[:, None, :], row_terms)
-    part = {at: terms[i] for i, at in enumerate(order)}
+    summed = lax.psum_scatter(terms, "dp", scatter_dimension=0, axis_index_groups=groups)
 
     scaled = (gates * grads.astype(F32)).astype(BF16)
-    queue = pieces(dot(rows, slopes[1], ((0,), (0,))).astype(BF16), 4)
-    queue += pieces(dot(lows[1], scaled, ((0,), (0,))).astype(BF16), 3)
-    swapped = []
-    plus, minus = part[-half], part[ring - half - 1]
-    for step in range(half):
-        sent = [queue.pop(0)] if queue and step > 0 else []
-        plus, minus, *sent = lax.optimization_barrier((plus, minus, *sent))
-        at = half - 1 - step
-        plus = shift(plus, -2)
-        if step > 0:
-            minus = shift(minus, 2)
-        if sent:
-            got = swap(sent[0])
-            plus, minus, got = lax.optimization_barrier((plus, minus, got))
-            swapped.append(got)
-        if at > 0:
-            plus = plus + part[-at]
-        if step > 0 and at > 0:
-            minus = minus + part[at]
-    summed = plus + minus + part[0]
-    while queue:
-        swapped.append(swap(queue.pop(0)))
-    mate_first = jnp.concatenate(swapped[:4], axis=0)
-    mate_second = jnp.concatenate(swapped[4:], axis=0)
+    mate_first = swap(dot(rows, slopes[1], ((0,), (0,))).astype(BF16))
+    mate_second = swap(dot(lows[1], scaled, ((0,), (0,))).astype(BF16))
     grad_first = (dot(rows, slopes[0], ((0,), (0,))) + mate_first.astype(F32)).astype(BF16)
     grad_second = (dot(lows[0], scaled, ((0,), (0,))) + mate_second.astype(F32)).astype(BF16)
 

time: 337 us -> 286 us (0.85)
  starting transfers between devices: 201 us -> 42.2 us
  waiting for transfers between devices: 104 us -> 198 us
  between operations: 1.84 us -> 14.4 us
  other arithmetic: 5.28 us -> 8.83 us
    ppermute x30 -> x0, starting transfers between devices: 127 us -> none  [shift(): return lax.ppermute(values, 'dp', [(i, (i + by) % dp) for i in range(dp)])]
    all_gather x0 -> x1, waiting for transfers between devices: none -> 98.4 us  [body(): gathered = lax.all_gather(block, 'dp', axis=0, axis_index_groups=groups)]
    unnamed x0 -> x3, waiting for transfers between devices: none -> 78.4 us
    ppermute x30 -> x0, waiting for transfers between devices: 77.7 us -> none  [shift(): return lax.ppermute(values, 'dp', [(i, (i + by) % dp) for i in range(dp)])]
    ppermute x12 -> x4, starting transfers between devices: 39.9 us -> 10.6 us  [swap(): return lax.ppermute(values, 'dp', [(i, i ^ 1) for i in range(dp)])]
    ppermute x12 -> x4, waiting for transfers between devices: 15.5 us -> 11.5 us  [swap(): return lax.ppermute(values, 'dp', [(i, i ^ 1) for i in range(dp)])]
  transfers between devices with their start and end apart: 44 -> 8, of which waited for: 28 -> 5; matrix products, arithmetic and copies ran while one was open for 4% -> 6% of each run, Pallas kernels for 0% -> 0%
where the time goes in v3:
time: 286 us; the launch traced here: 285 us
  waiting for transfers between devices  198 us (69%)
  starting transfers between devices  42.2 us (15%)
  matrix products  16.6 us (6%)
  between operations  14.4 us (5%)
  other arithmetic  8.83 us (3%)
  local copies, waits for them, and re-layouts  4.75 us (2%)
    all_gather x1, waiting for transfers between devices, body(): gathered = lax.all_gather(block, 'dp', axis=0, axis_index_groups=groups)  98.4 us
    unnamed x3, waiting for transfers between devices  78.4 us
    all_to_all x1, starting transfers between devices, body(): lax.all_to_all(placed, 'expert', split_axis=0, concat_axis=0, tiled=True)  17.7 us
    dot_general x12, matrix products, dot(): lax.dot_general(left, right, ((dims[0], dims[1]), ((), ())), preferred_el...  16.6 us
    all_to_all x1, starting transfers between devices, body(): lax.all_to_all(grad_rows, 'expert', split_axis=0, concat_axis=0, tiled=True)  13.9 us
    ppermute x4, waiting for transfers between devices, swap(): return lax.ppermute(values, 'dp', [(i, i ^ 1) for i in range(dp)])  11.5 us
    ppermute x4, starting transfers between devices, swap(): return lax.ppermute(values, 'dp', [(i, i ^ 1) for i in range(dp)])  10.6 us
    all_to_all x1, waiting for transfers between devices, body(): lax.all_to_all(placed, 'expert', split_axis=0, concat_axis=0, tiled=True)  5.74 us
  transfers between devices with their start and end apart: 8, of which 5 were waited for; matrix products, arithmetic and copies ran while one was open for 6% of the time, Pallas kernels for 0%

profile of v3, /device:TPU:1, one launch (start us, length us, event | category | flops | bytes accessed | tf_op | source)
XLA Modules:
  0.0 285.2 jit_solution(11536148603015980910)
XLA Ops:
  7.2 0.0 copy-start
  7.2 0.8 compare_select_fusion
  8.0 1.2 fusion.3
  9.3 0.8 copy.33
  10.1 17.7 %all-to-all-start = ((bf16[32,24,104]{2,1,0:T(8,128)(2,1)}), bf16[32,24,104]{2,1,0:T(8,128)(2,1)S(1)}, u32[]{:S(2)}, u32[]{:S(2)}) async-start(bf16[32,24,104]{2,1,0:T(8,128)(2,1)} %bitcast), calls=%async_computation | async-start | bytes 393216 | tf_op jit(solution)/shard_map/all_to_all | solution.py:49
  27.7 0.0 all-gather.2.cloned.1.call-start
  27.8 0.7 convert_element_type.86
  28.5 1.9 select_reduce_fusion
  30.4 5.7 %all-to-all-done = bf16[32,24,104]{2,1,0:T(8,128)(2,1)S(1)} async-done(((bf16[32,24,104]{2,1,0:T(8,128)(2,1)}), bf16[32,24,104]{2,1,0:T(8,128)(2,1)S(1)}, u32[]{:S(2)}, u32[]{:S(2)}) %all-to-all-start) | async-done | bytes 159776 | tf_op jit(solution)/shard_map/all_to_all | solution.py:49
  36.1 0.2 reshape.117
  36.3 0.1 copy.46
  36.4 0.6 reshape.118
  37.0 0.8 broadcast_select_fusion.1
  37.8 0.0 all-gather.2.cloned.1.call-update
  37.8 0.0 reduce-scatter.4.cloned.1.call-start
  37.8 0.0 copy-done
  37.9 1.9 collective-permute-start
  39.8 3.4 %collective-permute-start.1 = (bf16[256,1664]{1,0:T(8,128)(2,1)}, bf16[256,1664]{1,0:T(8,128)(2,1)}, u32[]{:S(2)}, u32[]{:S(2)}) collective-permute-start(bf16[256,1664]{1,0:T(8,128)(2,1)} %bitcast.54), channel_id=1, source_target_pairs={{0,32},{32,0},{64,96},{96,64},{128,160},{160,128},{192,224},{224,1... | collective-permute-start | bytes 2555912 | tf_op jit(solution)/shard_map/ppermute | solution.py:35
  43.2 98.4 %all-gather.2.cloned.1.call-done = bf16[16,24,3328]{2,1,0:T(8,128)(2,1)} async-done(((bf16[1,24,3328]{2,1,0:T(8,128)(2,1)}), bf16[16,24,3328]{2,1,0:T(8,128)(2,1)}) %all-gather.2.cloned.1.call-update) | async-done | bytes 2555920 | tf_op jit(solution)/shard_map/all_gather | solution.py:58
  141.5 0.8 slice.40
  142.3 0.1 reshape.122
  142.4 0.0 copy-start.1
  142.4 0.0 copy-start.3
  142.4 2.2 fusion.19
  144.6 0.0 collective-permute-done
  144.6 0.0 copy-done.1
  144.6 0.7 fusion.17
  145.3 0.0 copy-done.3
  145.3 0.7 multiply_reduce_fusion.1
  146.0 0.0 collective-permute-done.1
  146.0 1.8 multiply_reduce_fusion
  147.8 0.1 add.58
  147.9 0.7 fusion.50
  148.6 0.7 convolution_add_fusion
  149.3 1.8 broadcast_select_fusion
  151.1 0.0 reduce-scatter.4.cloned.1.call-update
  151.1 0.0 copy-start.2
  151.1 2.2 convolution_convert_fusion.1
  153.4 1.9 collective-permute-start.2
  155.3 0.0 copy-done.2
  155.3 0.7 convolution_convert_fusion
  156.0 3.4 %collective-permute-start.3 = (bf16[256,1664]{1,0:T(8,128)(2,1)S(1)}, bf16[256,1664]{1,0:T(8,128)(2,1)S(1)}, u32[]{:S(2)}, u32[]{:S(2)}) collective-permute-start(bf16[256,1664]{1,0:T(8,128)(2,1)S(1)} %convolution_convert_fusion), channel_id=1, source_target_pairs={{0,32},{32,0},{64,96},{96,64},{128,160},{160,128},{192,224},{224,1... | collective-permute-start | bytes 2555912 | tf_op jit(solution)/shard_map/ppermute | solution.py:35
  159.4 11.5 %collective-permute-done.2 = bf16[1664,256]{1,0:T(8,128)(2,1)S(1)} collective-permute-done((bf16[1664,256]{1,0:T(8,128)(2,1)S(1)}, bf16[1664,256]{1,0:T(8,128)(2,1)S(1)}, u32[]{:S(2)}, u32[]{:S(2)}) %collective-permute-start.2) | collective-permute-done | bytes 852000 | tf_op jit(solution)/shard_map/ppermute | solution.py:35
  170.9 1.7 fusion.12
  172.6 78.4 %reduce-scatter.4.cloned.1.call-done = f32[1,24,1664]{2,1,0:T(8,128)} async-done(((f32[16,24,1664]{2,1,0:T(8,128)}), f32[1,24,1664]{2,1,0:T(8,128)}) %reduce-scatter.4.cloned.1.call-update) | async-done | bytes 159760
  251.0 0.9 convert.9
  251.9 0.6 convert_element_type.93
  252.4 0.9 convert_bitcast_fusion
  253.4 0.1 fusion.40
  253.5 0.9 reshape.127
  254.4 13.9 %all-to-all-start.1 = ((bf16[32,2,624]{2,1,0:T(2,128)(2,1)}), bf16[32,2,624]{2,1,0:T(2,128)(2,1)S(1)}, u32[]{:S(2)}, u32[]{:S(2)}) async-start(bf16[32,2,624]{2,1,0:T(2,128)(2,1)} %reshape.127), calls=%async_computation.1 | async-start | bytes 163840 | tf_op jit(solution)/shard_map/all_to_all | solution.py:89
  268.3 0.0 collective-permute-done.3
  268.3 2.9 %fusion.13 = bf16[1,256,1664]{2,1,0:T(8,128)(2,1)} fusion(bf16[256,1664]{1,0:T(8,128)(2,1)S(1)} %collective-permute-done.3, f32[384]{0:T(512)S(1)} %reshape.122, bf16[384,3328]{1,0:T(8,128)(2,1)} %bitcast.48, f32[384,256]{0,1:T(8,128)S(1)} %fusion.19), kind=kOutput, calls=%fused_computation.24 | convolution fusion | flops 330842112 | bytes 3376640 | tf_op jit(solution)/shard_map/dot_general | solution.py:19
  271.3 4.4 %all-to-all-done.1 = bf16[32,2,624]{2,1,0:T(2,128)(2,1)S(1)} async-done(((bf16[32,2,624]{2,1,0:T(2,128)(2,1)}), bf16[32,2,624]{2,1,0:T(2,128)(2,1)S(1)}, u32[]{:S(2)}, u32[]{:S(2)}) %all-to-all-start.1) | async-done | bytes 79904 | tf_op jit(solution)/shard_map/all_to_all | solution.py:89
  275.7 0.3 reshape.128
  276.0 0.1 copy.40
  276.1 0.1 copy.38
  276.2 0.1 reshape.123
  276.3 0.4 select_reduce_fusion.2
  276.7 1.1 convolution_convert_fusion.2
  277.7 0.6 pad_maximum_fusion
  (14 shorter events, 0.1 us)
Async XLA Ops:
  7.2 30.7 %copy-start = (bf16[1,1664,256]{2,1,0:T(8,128)(2,1)S(1)}, bf16[1,1664,256]{2,1,0:T(8,128)(2,1)}, u32[]{:S(2)}) copy-start(bf16[1,1664,256]{2,1,0:T(8,128)(2,1)} %param.14) | copy-start | bytes 2555908
  10.1 26.1 %all-to-all-start = ((bf16[32,24,104]{2,1,0:T(8,128)(2,1)}), bf16[32,24,104]{2,1,0:T(8,128)(2,1)S(1)}, u32[]{:S(2)}, u32[]{:S(2)}) async-start(bf16[32,24,104]{2,1,0:T(8,128)(2,1)} %bitcast), calls=%async_computation | async-start | bytes 393216 | tf_op jit(solution)/shard_map/all_to_all | solution.py:49
  27.7 113.8 %all-gather.2.cloned.1.call-start = ((), (), s32[]{:S(2)}) async-start(), calls=%async_computation.3 | async-start | bytes 2715648 | tf_op jit(solution)/shard_map/all_gather | solution.py:58
  37.8 213.2 %reduce-scatter.4.cloned.1.call-start = ((), (), s32[]{:S(2)}) async-start(), calls=%async_computation.4 | async-start | bytes 2715648
  37.9 106.7 %collective-permute-start = (bf16[1664,256]{1,0:T(8,128)(2,1)S(1)}, bf16[1664,256]{1,0:T(8,128)(2,1)S(1)}, u32[]{:S(2)}, u32[]{:S(2)}) collective-permute-start(bf16[1664,256]{1,0:T(8,128)(2,1)S(1)} %bitcast.41), channel_id=1, source_target_pairs={{0,32},{32,0},{64,96},{96,64},{128,160},{160,128},{192,224},{224,1... | collective-permute-start | bytes 2555912 | tf_op jit(solution)/shard_map/ppermute | solution.py:35
  39.8 106.2 %collective-permute-start.1 = (bf16[256,1664]{1,0:T(8,128)(2,1)}, bf16[256,1664]{1,0:T(8,128)(2,1)}, u32[]{:S(2)}, u32[]{:S(2)}) collective-permute-start(bf16[256,1664]{1,0:T(8,128)(2,1)} %bitcast.54), channel_id=1, source_target_pairs={{0,32},{32,0},{64,96},{96,64},{128,160},{160,128},{192,224},{224,1... | collective-permute-start | bytes 2555912 | tf_op jit(solution)/shard_map/ppermute | solution.py:35
  142.4 2.2 copy-start.1
  142.4 2.9 %copy-start.3 = (bf16[1,256,1664]{2,1,0:T(8,128)(2,1)S(1)}, bf16[1,256,1664]{2,1,0:T(8,128)(2,1)}, u32[]{:S(2)}) copy-start(bf16[1,256,1664]{2,1,0:T(8,128)(2,1)} %param.15) | copy-start | bytes 2555908
  151.1 4.2 %copy-start.2 = (bf16[16,24,3328]{2,1,0:T(8,128)(2,1)S(1)}, bf16[16,24,3328]{2,1,0:T(8,128)(2,1)}, u32[]{:S(2)}) copy-start(bf16[16,24,3328]{2,1,0:T(8,128)(2,1)} %all-gather.2.cloned.1.call-done) | copy-start | bytes 7667716
  153.4 17.5 %collective-permute-start.2 = (bf16[1664,256]{1,0:T(8,128)(2,1)S(1)}, bf16[1664,256]{1,0:T(8,128)(2,1)S(1)}, u32[]{:S(2)}, u32[]{:S(2)}) collective-permute-start(bf16[1664,256]{1,0:T(8,128)(2,1)S(1)} %convolution_convert_fusion.1), channel_id=1, source_target_pairs={{0,32},{32,0},{64,96},{96,64},{128,160},{160,128},{192,224},{224,1... | collective-permute-start | bytes 2555912 | tf_op jit(solution)/shard_map/ppermute | solution.py:35
  156.0 112.3 %collective-permute-start.3 = (bf16[256,1664]{1,0:T(8,128)(2,1)S(1)}, bf16[256,1664]{1,0:T(8,128)(2,1)S(1)}, u32[]{:S(2)}, u32[]{:S(2)}) collective-permute-start(bf16[256,1664]{1,0:T(8,128)(2,1)S(1)} %convolution_convert_fusion), channel_id=1, source_target_pairs={{0,32},{32,0},{64,96},{96,64},{128,160},{160,128},{192,224},{224,1... | collective-permute-start | bytes 2555912 | tf_op jit(solution)/shard_map/ppermute | solution.py:35
  254.4 21.3 %all-to-all-start.1 = ((bf16[32,2,624]{2,1,0:T(2,128)(2,1)}), bf16[32,2,624]{2,1,0:T(2,128)(2,1)S(1)}, u32[]{:S(2)}, u32[]{:S(2)}) async-start(bf16[32,2,624]{2,1,0:T(2,128)(2,1)} %reshape.127), calls=%async_computation.1 | async-start | bytes 163840 | tf_op jit(solution)/shard_map/all_to_all | solution.py:89
Sparse Core Ops, SparseCore 0:
  37.9 103.5 all-gather.1
  151.3 99.6 reduce-scatter.3

commit v4 on v3

--- a/solution.py
+++ b/solution.py
@@ -40,14 +40,15 @@
     kept = kept_mask == 1
     target = jnp.where(kept, route_ids * pad + route_slots, -1)
     slots = jnp.arange(experts * pad, dtype=jnp.int32)
-    both = jnp.concatenate([tokens, cotangent], axis=1)
+    lanes = (2 * piece + 127) // 128 * 128
+    both = jnp.pad(jnp.concatenate([tokens, cotangent], axis=1), ((0, 0), (0, lanes - 2 * piece)))
     spread = jnp.zeros((experts * pad, tok_rows), jnp.bool_)
     for k in range(top):
         spread = spread | (slots[:, None] == target[None, :, k])
     placed = dot(spread.astype(BF16), both, ((1,), (0,))).astype(BF16)
-    placed = placed.reshape(experts, pad, 2 * piece)
+    placed = placed.reshape(experts, pad, lanes)
     arrived = lax.all_to_all(placed, "expert", split_axis=0, concat_axis=0, tiled=True)
-    arrived = arrived.reshape(experts, pad, 2, piece).transpose(1, 2, 0, 3).reshape(pad, 2 * width)
+    arrived = arrived[:, :, : 2 * piece].reshape(experts, pad, 2, piece).transpose(1, 2, 0, 3).reshape(pad, 2 * width)
 
     own_slots = jnp.arange(2 * width, dtype=jnp.int32)
     hit = (target[:, :, None] == me * pad + own_slots[None, None, :]) & (own_slots < cap)[None, None, :]
@@ -82,21 +83,19 @@
     grad_first = (dot(rows, slopes[0], ((0,), (0,))) + mate_first.astype(F32)).astype(BF16)
     grad_second = (dot(lows[0], scaled, ((0,), (0,))) + mate_second.astype(F32)).astype(BF16)
 
-    slot_gates = jnp.pad(summed[cap, :cap].astype(BF16), (0, piece - cap))
     grad_rows = summed.astype(BF16).reshape(pad, experts, piece).transpose(1, 0, 2)
-    spare_slot = lax.broadcasted_iota(jnp.int32, (1, pad, 1), 1) == cap
-    grad_rows = jnp.where(spare_slot, slot_gates[None, None, :], grad_rows)
+    slot_gates = jnp.pad(grad_rows[0, cap, :cap], (0, pad - cap))
+    out_lanes = (piece + 1 + 127) // 128 * 128
+    grad_rows = jnp.pad(grad_rows, ((0, 0), (0, 0), (0, out_lanes - piece)))
+    lane = lax.broadcasted_iota(jnp.int32, (1, 1, out_lanes), 2)
+    grad_rows = jnp.where(lane == piece, slot_gates[None, :, None], grad_rows)
     returned = lax.all_to_all(grad_rows, "expert", split_axis=0, concat_axis=0, tiled=True)
-    gates_back = jnp.pad(returned[:, cap, :cap], ((0, 0), (0, pad - cap))).reshape(experts * pad)
-    returned = returned.reshape(experts * pad, piece)
-    gather = jnp.zeros((tok_rows, experts * pad), jnp.bool_)
-    gate_out = []
-    for k in range(top):
-        match = target[:, k, None] == slots[None, :]
-        gather = gather | match
-        gate_out.append(jnp.sum(jnp.where(match, gates_back.astype(F32)[None, :], 0.0), axis=1))
-    token_grads = dot(gather.astype(BF16), returned, ((1,), (0,))).astype(BF16)
-    return token_grads, jnp.stack(gate_out, axis=1), grad_first[None], grad_second[None]
+    returned = returned.reshape(experts * pad, out_lanes)
+    spots = jnp.concatenate([target[:, k] for k in range(top)], axis=0)
+    match = (spots[:, None] == slots[None, :]).astype(BF16)
+    taken = dot(match, returned, ((1,), (0,))).reshape(top, tok_rows, out_lanes)
+    token_grads = jnp.sum(taken[:, :, :piece], axis=0).astype(BF16)
+    return token_grads, taken[:, :, piece].T, grad_first[None], grad_second[None]
 
 
 def solution(mesh):

time: 286 us -> 286 us (level)
  matrix products: 16.6 us -> 20 us
    dot_general x12, matrix products: 16.6 us -> 20 us  [dot(): lax.dot_general(left, right, ((dims[0], dims[1]), ((), ())), preferred_el...]
  transfers between devices with their start and end apart: 8 -> 8, of which waited for: 5 -> 5; matrix products, arithmetic and copies ran while one was open for 6% -> 7% of each run, Pallas kernels for 0% -> 0%
where the time goes in v4:
time: 286 us; the launch traced here: 285 us
  waiting for transfers between devices  199 us (70%)
  starting transfers between devices  40.8 us (14%)
  matrix products  20 us (7%)
  between operations  14.3 us (5%)
  other arithmetic  7.03 us (2%)
  local copies, waits for them, and re-layouts  4.87 us (2%)
    all_gather x1, waiting for transfers between devices, body(): gathered = lax.all_gather(block, 'dp', axis=0, axis_index_groups=groups)  98.6 us
    unnamed x3, waiting for transfers between devices  77.6 us
    dot_general x12, matrix products, dot(): lax.dot_general(left, right, ((dims[0], dims[1]), ((), ())), preferred_el...  20 us
    all_to_all x1, starting transfers between devices, body(): lax.all_to_all(placed, 'expert', split_axis=0, concat_axis=0, tiled=True)  17.7 us
    all_to_all x1, starting transfers between devices, body(): lax.all_to_all(grad_rows, 'expert', split_axis=0, concat_axis=0, tiled=True)  12.5 us
    ppermute x4, waiting for transfers between devices, swap(): return lax.ppermute(values, 'dp', [(i, i ^ 1) for i in range(dp)])  11.2 us
    ppermute x4, starting transfers between devices, swap(): return lax.ppermute(values, 'dp', [(i, i ^ 1) for i in range(dp)])  10.6 us
    all_to_all x1, waiting for transfers between devices, body(): lax.all_to_all(placed, 'expert', split_axis=0, concat_axis=0, tiled=True)  5.74 us
  transfers between devices with their start and end apart: 8, of which 5 were waited for; matrix products, arithmetic and copies ran while one was open for 7% of the time, Pallas kernels for 0%

profile of v4, /device:TPU:1, one launch (start us, length us, event | category | flops | bytes accessed | tf_op | source)
XLA Modules:
  0.0 285.5 jit_solution(15064236585467809105)
XLA Ops:
  7.2 0.0 copy-start
  7.2 0.8 compare_select_fusion
  8.0 1.9 fusion.6
  9.9 17.7 %all-to-all-start = ((bf16[32,24,128]{2,1,0:T(8,128)(2,1)}), bf16[32,24,128]{2,1,0:T(8,128)(2,1)S(1)}, u32[]{:S(2)}, u32[]{:S(2)}) async-start(bf16[32,24,128]{2,1,0:T(8,128)(2,1)} %bitcast.1), calls=%async_computation | async-start | bytes 393216 | tf_op jit(solution)/shard_map/all_to_all | solution.py:50
  27.5 0.0 all-gather.2.cloned.1.call-start
  27.6 0.7 convert_element_type.75
  28.3 1.9 select_reduce_fusion
  30.2 5.7 %all-to-all-done = bf16[32,24,128]{2,1,0:T(8,128)(2,1)S(1)} async-done(((bf16[32,24,128]{2,1,0:T(8,128)(2,1)}), bf16[32,24,128]{2,1,0:T(8,128)(2,1)S(1)}, u32[]{:S(2)}, u32[]{:S(2)}) %all-to-all-start) | async-done | bytes 196640 | tf_op jit(solution)/shard_map/all_to_all | solution.py:50
  35.9 0.2 reshape.138
  36.1 0.1 copy.27
  36.2 0.6 reshape.139
  36.8 0.8 broadcast_select_fusion.1
  37.6 0.0 all-gather.2.cloned.1.call-update
  37.6 0.0 reduce-scatter.4.cloned.1.call-start
  37.6 0.0 copy-done
  37.6 1.9 collective-permute-start
  39.6 3.4 %collective-permute-start.1 = (bf16[256,1664]{1,0:T(8,128)(2,1)}, bf16[256,1664]{1,0:T(8,128)(2,1)}, u32[]{:S(2)}, u32[]{:S(2)}) collective-permute-start(bf16[256,1664]{1,0:T(8,128)(2,1)} %bitcast.58), channel_id=1, source_target_pairs={{0,32},{32,0},{64,96},{96,64},{128,160},{160,128},{192,224},{224,1... | collective-permute-start | bytes 2555912 | tf_op jit(solution)/shard_map/ppermute | solution.py:35
  42.9 98.6 %all-gather.2.cloned.1.call-done = bf16[16,24,3328]{2,1,0:T(8,128)(2,1)} async-done(((bf16[1,24,3328]{2,1,0:T(8,128)(2,1)}), bf16[16,24,3328]{2,1,0:T(8,128)(2,1)}) %all-gather.2.cloned.1.call-update) | async-done | bytes 2555920 | tf_op jit(solution)/shard_map/all_gather | solution.py:59
  141.6 0.8 slice.48
  142.4 0.1 reshape.143
  142.5 0.0 copy-start.1
  142.5 0.0 copy-start.3
  142.5 2.1 fusion.21
  144.6 0.0 collective-permute-done
  144.6 0.0 copy-done.1
  144.7 0.7 fusion.19
  145.4 0.0 copy-done.3
  145.4 0.7 multiply_reduce_fusion.1
  146.0 0.0 collective-permute-done.1
  146.0 1.8 multiply_reduce_fusion
  147.9 0.1 add.60
  148.0 0.7 fusion.56
  148.7 0.7 convolution_add_fusion
  149.4 1.8 broadcast_select_fusion
  151.2 0.0 reduce-scatter.4.cloned.1.call-update
  151.2 3.0 %convolution_convert_fusion.1 = bf16[1664,256]{1,0:T(8,128)(2,1)} fusion(bf16[384,3328]{1,0:T(8,128)(2,1)} %bitcast.51, f32[384,256]{0,1:T(8,128)S(1)} %fusion.19, f32[384,256]{0,1:T(8,128)S(1)} %get-tuple-element.17, f32[384]{0:T(512)S(1)} %reshape.143), kind=kOutput, calls=%fused_computation.3 | convolution fusion | flops 328663040 | bytes 2917888 | tf_op jit(solution)/shard_map/dot_general | solution.py:19
  154.2 1.9 collective-permute-start.2
  156.1 0.1 pad_add_fusion
  156.2 0.1 eq.102
  156.2 0.0 copy-start.2
  156.2 2.2 convolution_convert_fusion
  158.4 3.4 %collective-permute-start.3 = (bf16[256,1664]{1,0:T(8,128)(2,1)S(1)}, bf16[256,1664]{1,0:T(8,128)(2,1)S(1)}, u32[]{:S(2)}, u32[]{:S(2)}) collective-permute-start(bf16[256,1664]{1,0:T(8,128)(2,1)S(1)} %convolution_convert_fusion), channel_id=1, source_target_pairs={{0,32},{32,0},{64,96},{96,64},{128,160},{160,128},{192,224},{224,1... | collective-permute-start | bytes 2555912 | tf_op jit(solution)/shard_map/ppermute | solution.py:35
  161.8 11.2 %collective-permute-done.2 = bf16[1664,256]{1,0:T(8,128)(2,1)} collective-permute-done((bf16[1664,256]{1,0:T(8,128)(2,1)}, bf16[1664,256]{1,0:T(8,128)(2,1)}, u32[]{:S(2)}, u32[]{:S(2)}) %collective-permute-start.2) | collective-permute-done | bytes 852000 | tf_op jit(solution)/shard_map/ppermute | solution.py:35
  173.0 0.0 copy-done.2
  173.0 2.8 fusion.14
  175.8 77.6 %reduce-scatter.4.cloned.1.call-done = f32[1,24,1664]{2,1,0:T(8,128)} async-done(((f32[16,24,1664]{2,1,0:T(8,128)}), f32[1,24,1664]{2,1,0:T(8,128)}) %reduce-scatter.4.cloned.1.call-update) | async-done | bytes 159760
  253.4 0.9 convert_element_type.81
  254.3 0.6 convert_element_type.82
  254.9 0.1 pad_select_fusion
  255.0 0.8 copy.29
  255.8 12.5 %all-to-all-start.1 = ((bf16[32,24,128]{2,1,0:T(8,128)(2,1)}), bf16[32,24,128]{2,1,0:T(8,128)(2,1)S(1)}, u32[]{:S(2)}, u32[]{:S(2)}) async-start(bf16[32,24,128]{2,1,0:T(8,128)(2,1)} %copy.29), calls=%async_computation.1 | async-start | bytes 393216 | tf_op jit(solution)/shard_map/all_to_all | solution.py:92
  268.3 0.0 collective-permute-done.3
  268.3 2.9 %fusion.15 = bf16[1,256,1664]{2,1,0:T(8,128)(2,1)} fusion(bf16[256,1664]{1,0:T(8,128)(2,1)S(1)} %collective-permute-done.3, f32[384]{0:T(512)S(1)} %reshape.143, bf16[384,3328]{1,0:T(8,128)(2,1)} %bitcast.53, f32[384,256]{0,1:T(8,128)S(1)} %fusion.21), kind=kOutput, calls=%fused_computation.22 | convolution fusion | flops 330842112 | bytes 3376640 | tf_op jit(solution)/shard_map/dot_general | solution.py:19
  271.2 5.3 %all-to-all-done.1 = bf16[32,24,128]{2,1,0:T(8,128)(2,1)S(1)} async-done(((bf16[32,24,128]{2,1,0:T(8,128)(2,1)}), bf16[32,24,128]{2,1,0:T(8,128)(2,1)S(1)}, u32[]{:S(2)}, u32[]{:S(2)}) %all-to-all-start.1) | async-done | bytes 196640 | tf_op jit(solution)/shard_map/all_to_all | solution.py:92
  276.5 0.5 fusion.1
  277.0 0.9 slice_reduce_fusion
  277.9 0.7 copy.30
  (12 shorter events, 0.1 us)
Async XLA Ops:
  7.2 30.5 %copy-start = (bf16[1,1664,256]{2,1,0:T(8,128)(2,1)S(1)}, bf16[1,1664,256]{2,1,0:T(8,128)(2,1)}, u32[]{:S(2)}) copy-start(bf16[1,1664,256]{2,1,0:T(8,128)(2,1)} %param.14) | copy-start | bytes 2555908
  9.9 26.1 %all-to-all-start = ((bf16[32,24,128]{2,1,0:T(8,128)(2,1)}), bf16[32,24,128]{2,1,0:T(8,128)(2,1)S(1)}, u32[]{:S(2)}, u32[]{:S(2)}) async-start(bf16[32,24,128]{2,1,0:T(8,128)(2,1)} %bitcast.1), calls=%async_computation | async-start | bytes 393216 | tf_op jit(solution)/shard_map/all_to_all | solution.py:50
  27.5 114.0 %all-gather.2.cloned.1.call-start = ((), (), s32[]{:S(2)}) async-start(), calls=%async_computation.3 | async-start | bytes 2715648 | tf_op jit(solution)/shard_map/all_gather | solution.py:59
  37.6 215.8 %reduce-scatter.4.cloned.1.call-start = ((), (), s32[]{:S(2)}) async-start(), calls=%async_computation.4 | async-start | bytes 2715648
  37.6 107.0 %collective-permute-start = (bf16[1664,256]{1,0:T(8,128)(2,1)S(1)}, bf16[1664,256]{1,0:T(8,128)(2,1)S(1)}, u32[]{:S(2)}, u32[]{:S(2)}) collective-permute-start(bf16[1664,256]{1,0:T(8,128)(2,1)S(1)} %bitcast.42), channel_id=1, source_target_pairs={{0,32},{32,0},{64,96},{96,64},{128,160},{160,128},{192,224},{224,1... | collective-permute-start | bytes 2555912 | tf_op jit(solution)/shard_map/ppermute | solution.py:35
  39.6 106.5 %collective-permute-start.1 = (bf16[256,1664]{1,0:T(8,128)(2,1)}, bf16[256,1664]{1,0:T(8,128)(2,1)}, u32[]{:S(2)}, u32[]{:S(2)}) collective-permute-start(bf16[256,1664]{1,0:T(8,128)(2,1)} %bitcast.58), channel_id=1, source_target_pairs={{0,32},{32,0},{64,96},{96,64},{128,160},{160,128},{192,224},{224,1... | collective-permute-start | bytes 2555912 | tf_op jit(solution)/shard_map/ppermute | solution.py:35
  142.5 2.2 copy-start.1
  142.5 2.9 %copy-start.3 = (bf16[1,256,1664]{2,1,0:T(8,128)(2,1)S(1)}, bf16[1,256,1664]{2,1,0:T(8,128)(2,1)}, u32[]{:S(2)}) copy-start(bf16[1,256,1664]{2,1,0:T(8,128)(2,1)} %param.15) | copy-start | bytes 2555908
  154.2 18.8 %collective-permute-start.2 = (bf16[1664,256]{1,0:T(8,128)(2,1)}, bf16[1664,256]{1,0:T(8,128)(2,1)}, u32[]{:S(2)}, u32[]{:S(2)}) collective-permute-start(bf16[1664,256]{1,0:T(8,128)(2,1)} %convolution_convert_fusion.1), channel_id=1, source_target_pairs={{0,32},{32,0},{64,96},{96,64},{128,160},{160,128},{192,224},{224,1... | collective-permute-start | bytes 2555912 | tf_op jit(solution)/shard_map/ppermute | solution.py:35
  156.2 16.7 %copy-start.2 = (bf16[16,24,3328]{2,1,0:T(8,128)(2,1)S(1)}, bf16[16,24,3328]{2,1,0:T(8,128)(2,1)}, u32[]{:S(2)}) copy-start(bf16[16,24,3328]{2,1,0:T(8,128)(2,1)} %all-gather.2.cloned.1.call-done) | copy-start | bytes 7667716
  158.4 109.9 %collective-permute-start.3 = (bf16[256,1664]{1,0:T(8,128)(2,1)S(1)}, bf16[256,1664]{1,0:T(8,128)(2,1)S(1)}, u32[]{:S(2)}, u32[]{:S(2)}) collective-permute-start(bf16[256,1664]{1,0:T(8,128)(2,1)S(1)} %convolution_convert_fusion), channel_id=1, source_target_pairs={{0,32},{32,0},{64,96},{96,64},{128,160},{160,128},{192,224},{224,1... | collective-permute-start | bytes 2555912 | tf_op jit(solution)/shard_map/ppermute | solution.py:35
  255.8 20.8 %all-to-all-start.1 = ((bf16[32,24,128]{2,1,0:T(8,128)(2,1)}), bf16[32,24,128]{2,1,0:T(8,128)(2,1)S(1)}, u32[]{:S(2)}, u32[]{:S(2)}) async-start(bf16[32,24,128]{2,1,0:T(8,128)(2,1)} %copy.29), calls=%async_computation.1 | async-start | bytes 393216 | tf_op jit(solution)/shard_map/all_to_all | solution.py:92
Sparse Core Ops, SparseCore 0:
  37.7 103.8 all-gather.1
  151.3 102.0 reduce-scatter.3

commit v5 on v4

--- a/solution.py
+++ b/solution.py
@@ -93,9 +93,9 @@
     returned = returned.reshape(experts * pad, out_lanes)
     spots = jnp.concatenate([target[:, k] for k in range(top)], axis=0)
     match = (spots[:, None] == slots[None, :]).astype(BF16)
-    taken = dot(match, returned, ((1,), (0,))).reshape(top, tok_rows, out_lanes)
-    token_grads = jnp.sum(taken[:, :, :piece], axis=0).astype(BF16)
-    return token_grads, taken[:, :, piece].T, grad_first[None], grad_second[None]
+    taken = dot(returned, match, ((0,), (1,))).reshape(out_lanes, top, tok_rows)
+    token_grads = jnp.sum(taken[:piece], axis=1).astype(BF16).T
+    return token_grads, taken[piece].T, grad_first[None], grad_second[None]
 
 
 def solution(mesh):

time: 286 us -> 287 us (level)
  matrix products: 20 us -> 16.7 us
    dot_general x12, matrix products: 20 us -> 16.7 us  [dot(): lax.dot_general(left, right, ((dims[0], dims[1]), ((), ())), preferred_el...]
  transfers between devices with their start and end apart: 8 -> 8, of which waited for: 5 -> 5; matrix products, arithmetic and copies ran while one was open for 7% -> 6% of each run, Pallas kernels for 0% -> 0%
where the time goes in v5:
time: 287 us
  waiting for transfers between devices  201 us (70%)
  starting transfers between devices  42.4 us (15%)
  matrix products  16.7 us (6%)
  between operations  14.4 us (5%)
  other arithmetic  7.82 us (3%)
  local copies, waits for them, and re-layouts  4.02 us (1%)
    all_gather x1, waiting for transfers between devices, body(): gathered = lax.all_gather(block, 'dp', axis=0, axis_index_groups=groups)  98.6 us
    unnamed x3, waiting for transfers between devices  79.2 us
    all_to_all x1, starting transfers between devices, body(): lax.all_to_all(placed, 'expert', split_axis=0, concat_axis=0, tiled=True)  17.7 us
    dot_general x12, matrix products, dot(): lax.dot_general(left, right, ((dims[0], dims[1]), ((), ())), preferred_el...  16.7 us
    all_to_all x1, starting transfers between devices, body(): lax.all_to_all(grad_rows, 'expert', split_axis=0, concat_axis=0, tiled=True)  14.1 us
    ppermute x4, waiting for transfers between devices, swap(): return lax.ppermute(values, 'dp', [(i, i ^ 1) for i in range(dp)])  12.4 us
    ppermute x4, starting transfers between devices, swap(): return lax.ppermute(values, 'dp', [(i, i ^ 1) for i in range(dp)])  10.6 us
  transfers between devices with their start and end apart: 8, of which 5 were waited for; matrix products, arithmetic and copies ran while one was open for 6% of the time, Pallas kernels for 0%

profile of v5, /device:TPU:1, one launch (start us, length us, event | category | flops | bytes accessed | tf_op | source)
XLA Modules:
  0.0 286.6 jit_solution(8001466389083068695)
XLA Ops:
  7.2 0.0 copy-start
  7.2 0.8 compare_select_fusion
  8.0 1.9 fusion.4
  9.9 17.7 %all-to-all-start = ((bf16[32,24,128]{2,1,0:T(8,128)(2,1)}), bf16[32,24,128]{2,1,0:T(8,128)(2,1)S(1)}, u32[]{:S(2)}, u32[]{:S(2)}) async-start(bf16[32,24,128]{2,1,0:T(8,128)(2,1)} %bitcast), calls=%async_computation | async-start | bytes 393216 | tf_op jit(solution)/shard_map/all_to_all | solution.py:50
  27.5 0.0 all-gather.2.cloned.1.call-start
  27.6 0.7 convert_element_type.79
  28.3 1.9 select_reduce_fusion
  30.2 5.7 %all-to-all-done = bf16[32,24,128]{2,1,0:T(8,128)(2,1)S(1)} async-done(((bf16[32,24,128]{2,1,0:T(8,128)(2,1)}), bf16[32,24,128]{2,1,0:T(8,128)(2,1)S(1)}, u32[]{:S(2)}, u32[]{:S(2)}) %all-to-all-start) | async-done | bytes 196640 | tf_op jit(solution)/shard_map/all_to_all | solution.py:50
  35.9 0.2 reshape.118
  36.1 0.1 copy.25
  36.2 0.6 reshape.119
  36.8 0.8 broadcast_select_fusion.1
  37.6 0.0 all-gather.2.cloned.1.call-update
  37.6 0.0 reduce-scatter.4.cloned.1.call-start
  37.6 0.0 copy-done
  37.6 1.9 collective-permute-start
  39.6 3.4 %collective-permute-start.1 = (bf16[256,1664]{1,0:T(8,128)(2,1)}, bf16[256,1664]{1,0:T(8,128)(2,1)}, u32[]{:S(2)}, u32[]{:S(2)}) collective-permute-start(bf16[256,1664]{1,0:T(8,128)(2,1)} %bitcast.57), channel_id=1, source_target_pairs={{0,32},{32,0},{64,96},{96,64},{128,160},{160,128},{192,224},{224,1... | collective-permute-start | bytes 2555912 | tf_op jit(solution)/shard_map/ppermute | solution.py:35
  42.9 98.6 %all-gather.2.cloned.1.call-done = bf16[16,24,3328]{2,1,0:T(8,128)(2,1)} async-done(((bf16[1,24,3328]{2,1,0:T(8,128)(2,1)}), bf16[16,24,3328]{2,1,0:T(8,128)(2,1)}) %all-gather.2.cloned.1.call-update) | async-done | bytes 2555920 | tf_op jit(solution)/shard_map/all_gather | solution.py:59
  141.6 0.8 slice.53
  142.4 0.1 reshape.123
  142.5 0.0 copy-start.1
  142.5 0.0 copy-start.3
  142.5 2.1 fusion.19
  144.6 0.0 collective-permute-done
  144.6 0.0 copy-done.1
  144.7 0.7 fusion.17
  145.4 0.0 copy-done.3
  145.4 0.7 multiply_reduce_fusion.1
  146.0 0.0 collective-permute-done.1
  146.0 1.8 multiply_reduce_fusion
  147.9 0.1 add.60
  148.0 0.7 fusion.54
  148.7 0.7 convolution_add_fusion
  149.4 1.8 broadcast_select_fusion
  151.2 0.0 reduce-scatter.4.cloned.1.call-update
  151.2 0.0 copy-start.2
  151.2 2.2 convolution_convert_fusion.1
  153.4 1.9 collective-permute-start.2
  155.3 0.1 pad_add_fusion
  155.4 0.0 copy-done.2
  155.4 0.7 convolution_convert_fusion
  156.2 3.4 %collective-permute-start.3 = (bf16[256,1664]{1,0:T(8,128)(2,1)S(1)}, bf16[256,1664]{1,0:T(8,128)(2,1)S(1)}, u32[]{:S(2)}, u32[]{:S(2)}) collective-permute-start(bf16[256,1664]{1,0:T(8,128)(2,1)S(1)} %convolution_convert_fusion), channel_id=1, source_target_pairs={{0,32},{32,0},{64,96},{96,64},{128,160},{160,128},{192,224},{224,1... | collective-permute-start | bytes 2555912 | tf_op jit(solution)/shard_map/ppermute | solution.py:35
  159.5 12.4 %collective-permute-done.2 = bf16[1664,256]{1,0:T(8,128)(2,1)S(1)} collective-permute-done((bf16[1664,256]{1,0:T(8,128)(2,1)S(1)}, bf16[1664,256]{1,0:T(8,128)(2,1)S(1)}, u32[]{:S(2)}, u32[]{:S(2)}) %collective-permute-start.2) | collective-permute-done | bytes 852000 | tf_op jit(solution)/shard_map/ppermute | solution.py:35
  171.9 1.7 fusion.12
  173.6 79.2 %reduce-scatter.4.cloned.1.call-done = f32[1,24,1664]{2,1,0:T(8,128)} async-done(((f32[16,24,1664]{2,1,0:T(8,128)}), f32[1,24,1664]{2,1,0:T(8,128)}) %reduce-scatter.4.cloned.1.call-update) | async-done | bytes 159760
  252.7 0.9 convert_element_type.85
  253.7 0.6 convert_element_type.86
  254.3 0.1 pad_select_fusion
  254.4 0.8 copy.27
  255.1 14.1 %all-to-all-start.1 = ((bf16[32,24,128]{2,1,0:T(8,128)(2,1)}), bf16[32,24,128]{2,1,0:T(8,128)(2,1)S(1)}, u32[]{:S(2)}, u32[]{:S(2)}) async-start(bf16[32,24,128]{2,1,0:T(8,128)(2,1)} %copy.27), calls=%async_computation.1 | async-start | bytes 393216 | tf_op jit(solution)/shard_map/all_to_all | solution.py:92
  269.2 0.0 collective-permute-done.3
  269.2 2.9 %fusion.13 = bf16[1,256,1664]{2,1,0:T(8,128)(2,1)} fusion(bf16[256,1664]{1,0:T(8,128)(2,1)S(1)} %collective-permute-done.3, f32[384]{0:T(512)S(1)} %reshape.123, bf16[384,3328]{1,0:T(8,128)(2,1)} %bitcast.51, f32[384,256]{0,1:T(8,128)S(1)} %fusion.19), kind=kOutput, calls=%fused_computation.21 | convolution fusion | flops 330842112 | bytes 3376640 | tf_op jit(solution)/shard_map/dot_general | solution.py:19
  272.1 5.3 %all-to-all-done.1 = bf16[32,24,128]{2,1,0:T(8,128)(2,1)S(1)} async-done(((bf16[32,24,128]{2,1,0:T(8,128)(2,1)}), bf16[32,24,128]{2,1,0:T(8,128)(2,1)S(1)}, u32[]{:S(2)}, u32[]{:S(2)}) %all-to-all-start.1) | async-done | bytes 196640 | tf_op jit(solution)/shard_map/all_to_all | solution.py:92
  277.5 0.6 fusion
  278.1 0.7 squeeze.18
  278.8 0.2 slice.45
  278.9 0.8 reduce_sum.39
  (13 shorter events, 0.1 us)
Async XLA Ops:
  7.2 30.5 %copy-start = (bf16[1,1664,256]{2,1,0:T(8,128)(2,1)S(1)}, bf16[1,1664,256]{2,1,0:T(8,128)(2,1)}, u32[]{:S(2)}) copy-start(bf16[1,1664,256]{2,1,0:T(8,128)(2,1)} %param.14) | copy-start | bytes 2555908
  9.9 26.1 %all-to-all-start = ((bf16[32,24,128]{2,1,0:T(8,128)(2,1)}), bf16[32,24,128]{2,1,0:T(8,128)(2,1)S(1)}, u32[]{:S(2)}, u32[]{:S(2)}) async-start(bf16[32,24,128]{2,1,0:T(8,128)(2,1)} %bitcast), calls=%async_computation | async-start | bytes 393216 | tf_op jit(solution)/shard_map/all_to_all | solution.py:50
  27.5 114.0 %all-gather.2.cloned.1.call-start = ((), (), s32[]{:S(2)}) async-start(), calls=%async_computation.3 | async-start | bytes 2715648 | tf_op jit(solution)/shard_map/all_gather | solution.py:59
  37.6 215.2 %reduce-scatter.4.cloned.1.call-start = ((), (), s32[]{:S(2)}) async-start(), calls=%async_computation.4 | async-start | bytes 2715648
  37.6 107.0 %collective-permute-start = (bf16[1664,256]{1,0:T(8,128)(2,1)S(1)}, bf16[1664,256]{1,0:T(8,128)(2,1)S(1)}, u32[]{:S(2)}, u32[]{:S(2)}) collective-permute-start(bf16[1664,256]{1,0:T(8,128)(2,1)S(1)} %bitcast.40), channel_id=1, source_target_pairs={{0,32},{32,0},{64,96},{96,64},{128,160},{160,128},{192,224},{224,1... | collective-permute-start | bytes 2555912 | tf_op jit(solution)/shard_map/ppermute | solution.py:35
  39.6 106.5 %collective-permute-start.1 = (bf16[256,1664]{1,0:T(8,128)(2,1)}, bf16[256,1664]{1,0:T(8,128)(2,1)}, u32[]{:S(2)}, u32[]{:S(2)}) collective-permute-start(bf16[256,1664]{1,0:T(8,128)(2,1)} %bitcast.57), channel_id=1, source_target_pairs={{0,32},{32,0},{64,96},{96,64},{128,160},{160,128},{192,224},{224,1... | collective-permute-start | bytes 2555912 | tf_op jit(solution)/shard_map/ppermute | solution.py:35
  142.5 2.2 copy-start.1
  142.5 2.9 %copy-start.3 = (bf16[1,256,1664]{2,1,0:T(8,128)(2,1)S(1)}, bf16[1,256,1664]{2,1,0:T(8,128)(2,1)}, u32[]{:S(2)}) copy-start(bf16[1,256,1664]{2,1,0:T(8,128)(2,1)} %param.15) | copy-start | bytes 2555908
  151.2 4.2 %copy-start.2 = (bf16[16,24,3328]{2,1,0:T(8,128)(2,1)S(1)}, bf16[16,24,3328]{2,1,0:T(8,128)(2,1)}, u32[]{:S(2)}) copy-start(bf16[16,24,3328]{2,1,0:T(8,128)(2,1)} %all-gather.2.cloned.1.call-done) | copy-start | bytes 7667716
  153.4 18.5 %collective-permute-start.2 = (bf16[1664,256]{1,0:T(8,128)(2,1)S(1)}, bf16[1664,256]{1,0:T(8,128)(2,1)S(1)}, u32[]{:S(2)}, u32[]{:S(2)}) collective-permute-start(bf16[1664,256]{1,0:T(8,128)(2,1)S(1)} %convolution_convert_fusion.1), channel_id=1, source_target_pairs={{0,32},{32,0},{64,96},{96,64},{128,160},{160,128},{192,224},{224,1... | collective-permute-start | bytes 2555912 | tf_op jit(solution)/shard_map/ppermute | solution.py:35
  156.2 113.0 %collective-permute-start.3 = (bf16[256,1664]{1,0:T(8,128)(2,1)S(1)}, bf16[256,1664]{1,0:T(8,128)(2,1)S(1)}, u32[]{:S(2)}, u32[]{:S(2)}) collective-permute-start(bf16[256,1664]{1,0:T(8,128)(2,1)S(1)} %convolution_convert_fusion), channel_id=1, source_target_pairs={{0,32},{32,0},{64,96},{96,64},{128,160},{160,128},{192,224},{224,1... | collective-permute-start | bytes 2555912 | tf_op jit(solution)/shard_map/ppermute | solution.py:35
  255.1 22.3 %all-to-all-start.1 = ((bf16[32,24,128]{2,1,0:T(8,128)(2,1)}), bf16[32,24,128]{2,1,0:T(8,128)(2,1)S(1)}, u32[]{:S(2)}, u32[]{:S(2)}) async-start(bf16[32,24,128]{2,1,0:T(8,128)(2,1)} %copy.27), calls=%async_computation.1 | async-start | bytes 393216 | tf_op jit(solution)/shard_map/all_to_all | solution.py:92
Sparse Core Ops, SparseCore 0:
  37.7 103.8 all-gather.1
  151.3 101.3 reduce-scatter.3
